TPU v7x, 128 devices: a whole 4x4x4 slice. The times are simulated.
128 devices in a mesh: branch: 32 (over z, x, core), tensor: 4 (over y).
Axes of the slice: x: 4, y: 4, z: 4, core: 2. Of those that a mesh axis runs over, the one named last changes fastest.
Arguments:
- inputs: bfloat16 [4, 512, 2048], P(None, 'branch'), may hold values from -6 to 6
- w_query: bfloat16 [2048, 2048], P(None, 'tensor'), may hold values from -0.125 to 0.125
- w_key: bfloat16 [2048, 2048], P(None, 'tensor'), may hold values from -0.125 to 0.125
- w_value: bfloat16 [2048, 4096], P(None, 'tensor'), may hold values from -0.125 to 0.125
- w_gate_z: bfloat16 [2048, 4096], P(None, 'tensor'), may hold values from -0.125 to 0.125
- w_beta: bfloat16 [2048, 32], P(None, 'tensor'), may hold values from -0.125 to 0.125
- w_decay: bfloat16 [2048, 32], P(None, 'tensor'), may hold values from -0.125 to 0.125
- conv_query: bfloat16 [4, 2048], P(None, 'tensor'), may hold values from -3 to 3
- conv_key: bfloat16 [4, 2048], P(None, 'tensor'), may hold values from -3 to 3
- conv_value: bfloat16 [4, 4096], P(None, 'tensor'), may hold values from -3 to 3
- decay_log: float32 [32], P('tensor'), may hold values from -3 to 1
- dt_bias: float32 [32], P('tensor'), may hold values from -1 to 1
- norm_gain: float32 [128], replicated, may hold values from 0.1 to 1.9
- w_out: bfloat16 [4096, 2048], P('tensor'), may hold values from -0.09375 to 0.09375
- state: bfloat16 [512, 32, 128, 128], P('branch', 'tensor'), may hold values from -4 to 4
- tail_query: bfloat16 [512, 3, 2048], P('branch', None, 'tensor'), may hold values from -6 to 6
- tail_key: bfloat16 [512, 3, 2048], P('branch', None, 'tensor'), may hold values from -6 to 6
- tail_value: bfloat16 [512, 3, 4096], P('branch', None, 'tensor'), may hold values from -6 to 6
- parents: int32 [512], P('branch'), may hold values from 0 to 511, as said below
Outputs:
- out_rows: bfloat16 [4, 512, 2048], P(None, 'branch', 'tensor')
- final_state: bfloat16 [512, 32, 128, 128], P('branch', 'tensor')
- final_tail_query: bfloat16 [512, 3, 2048], P('branch', None, 'tensor')
- final_tail_key: bfloat16 [512, 3, 2048], P('branch', None, 'tensor')
- final_tail_value: bfloat16 [512, 3, 4096], P('branch', None, 'tensor')
Inputs may be any that keep to these rules, and one draw needn't show every extreme that they name: `parents`: for every aligned block of 16 branches and every block of 16 branches, either none or exactly 1 of the first block's branches have their parent in the second block.
All inputs are finite; a program needn't handle non-finite values.
Results may differ from a plain program's by a relative error of at most 0.0059.
Values may be sent and summed in bfloat16 or wider, within the bound.
No kernel may reach another device: no remote copies, remote signals or barrier semaphores. Data moves between devices by JAX's collectives and lax.ppermute only.
A program may use at most 128 MiB of HBM per device.

v0:
```python
import jax
import jax.numpy as jnp
from jax import lax
from jax.experimental import pallas as pl
from jax.experimental.pallas import tpu as pltpu
from jax.sharding import PartitionSpec as P

DK = 128
DV = 128
HEADS = 8
KEYS = 4
ROWS = 16
TAPS = 4
WIDE = 3 * HEADS
SLIM = 2 * KEYS + HEADS
BODY = HEADS * DK
SLOT = BODY + (TAPS - 1) * SLIM
VMEM_BYTES = 48 * 1024 * 1024
CHUNK = 4
GROUP = 4
f32 = jnp.float32
bf16 = jnp.bfloat16


def split(value):
    high = value.astype(bf16).astype(f32)
    return high, value - high


def dot(left, right):
    return jnp.dot(left, right, preferred_element_type=f32)


def inner(left, right):
    return jnp.sum(left * right, axis=-1, keepdims=True)


def widening():
    row = lax.broadcasted_iota(jnp.int32, ((TAPS - 1) * WIDE, (TAPS - 1) * SLIM), 0)
    column = lax.broadcasted_iota(jnp.int32, ((TAPS - 1) * WIDE, (TAPS - 1) * SLIM), 1)
    tap, place = row // WIDE, row % WIDE
    origin = tap * SLIM + jnp.where(place < 2 * HEADS, place // 2, place - HEADS)
    return jnp.where(origin == column, 1.0, 0.0).astype(bf16)


def part_of(ref, index, first, count):
    return ref[pl.ds(index * ROWS * HEADS + first * HEADS, count * HEADS), :]


def find_vectors(window, conv_ref, vector_buf, value_buf):
    for first in range(0, ROWS, CHUNK):
        there = slice(first, first + CHUNK)
        for step in range(2):
            for kind in range(3):
                mixed = 0.0
                for tap in range(TAPS):
                    rows = window(kind, step + tap, first).reshape(CHUNK, HEADS, DV)
                    mixed = mixed + rows * conv_ref[kind, tap][None]
                mixed = mixed * jax.nn.sigmoid(mixed)
                if kind == 2:
                    value_buf[step, there] = mixed
                    continue
                unit = mixed * lax.rsqrt(inner(mixed, mixed) + 1e-06)
                if kind == 0:
                    unit = unit * DK ** (-0.5)
                place = 2 * step + 1 - kind
                vector_buf[there, place * HEADS : (place + 1) * HEADS, :] = unit


def recall(wait, memory, vector_buf, found_buf):
    head = lax.broadcasted_iota(jnp.int32, (HEADS, DV), 0)

    def one(row):
        high, low = split(vector_buf[row])
        left = jnp.concatenate([high, low], axis=0).astype(bf16)
        found = [jnp.zeros((HEADS, DV), f32)] * 4
        for h in range(0, HEADS, 2):
            pair = jnp.concatenate([memory(row, h), memory(row, h + 1)], axis=1)
            product = dot(left, pair)
            product = product[: 4 * HEADS] + product[4 * HEADS :]
            for i in range(4):
                block = product[i * HEADS : (i + 1) * HEADS]
                found[i] = jnp.where(head == h, block[:, :DV], found[i])
                found[i] = jnp.where(head == h + 1, block[:, DV:], found[i])
        found_buf[row] = jnp.concatenate(found, axis=0)

    def group(index, carry):
        for i in range(GROUP):
            wait(index * GROUP + i)
        for i in range(GROUP):
            one(index * GROUP + i)
        return carry

    lax.fori_loop(0, ROWS // GROUP, group, 0)


def finish(strength, decay, gate, vector_buf, value_buf, found_buf, normed_buf, update_ref):
    for first in range(0, ROWS, CHUNK):
        there = slice(first, first + CHUNK)

        def piece(ref, i):
            return ref[there, i * HEADS : (i + 1) * HEADS, :]

        def shaped(value):
            return value.reshape(CHUNK, HEADS, DV)

        key0, query0, key1, query1 = [piece(vector_buf, i) for i in range(4)]
        found0, found1, found2, found3 = [piece(found_buf, i) for i in range(4)]
        strength0, strength1 = [shaped(strength(step, first)) for step in range(2)]
        decay0, decay1 = [shaped(decay(step, first)) for step in range(2)]
        change0 = (value_buf[0, there] - decay0 * found0) * strength0
        read0 = decay0 * found1 + inner(query0, key0) * change0
        kept = decay0 * found2 + inner(key1, key0) * change0
        change1 = (value_buf[1, there] - decay1 * kept) * strength1
        kept = decay0 * found3 + inner(query1, key0) * change0
        read1 = decay1 * kept + inner(query1, key1) * change1
        for step, read in enumerate((read0, read1)):
            scale = lax.rsqrt(jnp.mean(read * read, axis=-1, keepdims=True) + 1e-06)
            normed = read * scale * shaped(gate(step, first))
            start = (step * ROWS + first) * HEADS
            normed_buf[start : start + CHUNK * HEADS, :] = normed.reshape(CHUNK * HEADS, DV)
        for i, value in enumerate((key0, key1, decay1 * change0, change1, decay0 * decay1)):
            update_ref[there, i * HEADS : (i + 1) * HEADS, :] = value


def flatten_heads(normed_buf, normed_ref):
    for h in range(HEADS):
        rows = normed_buf[pl.ds(h, 2 * ROWS, stride=HEADS), :]
        normed_ref[:, h * DV : (h + 1) * DV] = rows.astype(bf16)


def write_row(update, memory, store):
    key0, key1, change0, change1, decay = [
        update[i * HEADS : (i + 1) * HEADS] for i in range(5)
    ]
    (key0h, key0l), (key1h, key1l) = split(key0), split(key1)
    (change0h, change0l), (change1h, change1l) = split(change0), split(change1)
    left = jnp.concatenate([key0h, key0l, key0h, key1h, key1l, key1h], axis=0)
    left = left.T.astype(bf16)
    right = jnp.concatenate([change0h, change0h, change0l, change1h, change1h, change1l], axis=0)
    head = lax.broadcasted_iota(jnp.int32, right.shape, 0) % HEADS
    for h in range(0, HEADS, 2):
        pair = [jnp.where(head == h + i, right, 0.0).astype(bf16) for i in range(2)]
        added = dot(left, jnp.concatenate(pair, axis=1))
        for i in range(2):
            kept = memory(h + i).astype(f32) * decay[h + i : h + i + 1]
            store(h + i, (kept + added[:, i * DV : (i + 1) * DV]).astype(bf16))


def write_group(index, update_ref, memory_ref, target_ref):
    for i in range(GROUP):
        row = index * GROUP + i

        def store(h, value, row=row):
            target_ref[row, h * DK : (h + 1) * DK, :] = value

        write_row(
            update_ref[row], lambda h, row=row: memory_ref[row, h * DK : (h + 1) * DK, :], store
        )


def first_kernel(
    x, gain, tail_query, tail_key, tail_value, conv_query, conv_key, conv_value,
    w_query, w_key, w_value, w_gate, w_beta, w_decay, decay_log, dt_bias, state,
    late_query_ref, late_key_ref, late_value_ref, late_gate_ref, late_strength_ref, late_forget_ref,
    raw_ref, stored_ref, conv_ref, normed_ref, update_ref, state_buf,
    x_buf, gain_buf, tail_query_buf, tail_key_buf, tail_value_buf,
    conv_query_buf, conv_key_buf, conv_value_buf,
    query_buf, key_buf, value_weight_buf, gate_weight_buf, beta_buf, decay_buf, decay_ref, bias_ref,
    window_query, window_key, window_value, gate_all, strength_all, forget_all, stored_buf,
    vector_buf, value_buf, found_buf, normed_buf,
    small_sem, weight_sem, state_sem,
):
    rows = x_buf.shape[0]
    small = [
        pltpu.make_async_copy(source, target, small_sem.at[i])
        for i, (source, target) in enumerate(
            (
                (x, x_buf),
                (w_beta, beta_buf),
                (w_decay, decay_buf),
                (gain, gain_buf),
                (tail_query, tail_query_buf),
                (tail_key, tail_key_buf),
                (tail_value, tail_value_buf),
                (conv_query, conv_query_buf),
                (conv_key, conv_key_buf),
                (conv_value, conv_value_buf),
                (decay_log, decay_ref),
                (dt_bias, bias_ref),
            )
        )
    ]
    for copy in small:
        copy.start()

    def weights(j):
        pieces = (
            (w_query, query_buf, DK),
            (w_key, key_buf, DK),
            (w_value, value_weight_buf, 2 * DV),
            (w_gate, gate_weight_buf, 2 * DV),
        )
        copies = []
        for i, (hbm, buf, width) in enumerate(pieces):
            part = pl.ds(j * width, width)
            copies.append(
                pltpu.make_async_copy(hbm.at[:, part], buf.at[:, part], weight_sem.at[4 * j + i])
            )
        return copies

    def load(row):
        return pltpu.make_async_copy(state.at[row], state_buf.at[row], state_sem.at[row])

    def begin(j):
        if j < KEYS:
            for copy in weights(j):
                copy.start()
        elif j < KEYS + 2:
            for row in range((j - KEYS) * ROWS // 2, (j - KEYS + 1) * ROWS // 2):
                load(row).start()

    begin(0)
    begin(1)

    for copy in small:
        copy.wait()
    head = lax.broadcasted_iota(jnp.int32, (HEADS, DV), 0)
    rate, bias = jnp.zeros((HEADS, DV), f32), jnp.zeros((HEADS, DV), f32)
    for h in range(HEADS):
        rate = jnp.where(head == h, decay_ref[h], rate)
        bias = jnp.where(head == h, bias_ref[h], bias)
    rate = -jnp.exp(rate)
    x_all = x_buf[...]

    def spread(target, start, h, block):
        target[pl.ds(start * HEADS + h, block.shape[0], stride=HEADS), :] = block

    across = (((1,), (1,)), ((), ()))
    beta = lax.dot_general(x_all, beta_buf[...], across, preferred_element_type=f32)
    decay = lax.dot_general(x_all, decay_buf[...], across, preferred_element_type=f32)
    for h in range(HEADS):
        spread(strength_all, 0, h, jnp.broadcast_to(beta[:, h : h + 1], (rows, DV)))
        spread(forget_all, 0, h, jnp.broadcast_to(decay[:, h : h + 1], (rows, DV)))
    for first in range(0, rows, ROWS):
        there = slice(first * HEADS, (first + ROWS) * HEADS)
        strength_all[there] = jax.nn.sigmoid(strength_all[there])
        raised = forget_all[there].reshape(ROWS, HEADS, DV) + bias[None]
        forget = jnp.exp(rate[None] * jax.nn.softplus(raised))
        forget_all[there] = forget.reshape(ROWS * HEADS, DV)

    history = (TAPS - 1) * ROWS

    def place(window, h, before, fresh):
        spread(window, 0, h, before)
        spread(window, history, h, fresh)

    def keep(channel, before, fresh):
        after = jnp.concatenate([before[2 * ROWS :], fresh[: 2 * ROWS]], axis=0)
        for tap in range(TAPS - 1):
            stored_buf[pl.ds(tap * SLIM + channel, ROWS, stride=(TAPS - 1) * SLIM), :] = after[
                tap * ROWS : (tap + 1) * ROWS
            ]

    for kind, buf in enumerate((conv_query_buf, conv_key_buf, conv_value_buf)):
        wide = buf[...].astype(f32)
        for h in range(HEADS):
            channel = h if kind == 2 else h // 2
            taps = wide[:, channel * DV : (channel + 1) * DV]
            for tap in range(TAPS):
                conv_ref[kind, tap, h : h + 1, :] = taps[tap : tap + 1]

    for j in range(KEYS):
        for copy in weights(j):
            copy.wait()
        begin(j + 2)
        one, two = slice(j * DK, (j + 1) * DK), slice(2 * j * DV, 2 * (j + 1) * DV)
        query = dot(x_all, query_buf[:, one]).astype(bf16)
        key = dot(x_all, key_buf[:, one]).astype(bf16)
        value = dot(x_all, value_weight_buf[:, two]).astype(bf16)
        gate = dot(x_all, gate_weight_buf[:, two])
        raw_ref[:, j * DK : (j + 1) * DK] = query[2 * ROWS :]
        raw_ref[:, (KEYS + j) * DK : (KEYS + j + 1) * DK] = key[2 * ROWS :]
        raw_ref[:, 2 * (KEYS + j) * DK : 2 * (KEYS + j + 1) * DK] = value[2 * ROWS :]
        query, key, value = query.astype(f32), key.astype(f32), value.astype(f32)
        old_query = tail_query_buf[:, :, one].reshape(history, DK).astype(f32)
        old_key = tail_key_buf[:, :, one].reshape(history, DK).astype(f32)
        old_value = tail_value_buf[:, :, two].reshape(history, 2 * DV).astype(f32)
        gate = gate * jax.nn.sigmoid(gate)
        keep(j, old_query, query)
        keep(KEYS + j, old_key, key)
        for i in range(2):
            h, half = 2 * j + i, slice(i * DV, (i + 1) * DV)
            place(window_query, h, old_query, query)
            place(window_key, h, old_key, key)
            place(window_value, h, old_value[:, half], value[:, half])
            keep(2 * KEYS + h, old_value[:, half], value[:, half])
            spread(gate_all, 0, h, gate[:, half] * gain_buf[...])

    late = (history + 2 * ROWS) * HEADS
    late_query_ref[...] = window_query[late:, :]
    late_key_ref[...] = window_key[late:, :]
    late_value_ref[...] = window_value[late:, :]
    late_gate_ref[...] = gate_all[2 * ROWS * HEADS :, :]
    late_strength_ref[...] = strength_all[2 * ROWS * HEADS :, :]
    late_forget_ref[...] = forget_all[2 * ROWS * HEADS :, :]
    stored_ref[...] = stored_buf[...].reshape(stored_ref.shape).astype(bf16)

    windows = (window_query, window_key, window_value)
    find_vectors(
        lambda kind, tap, first: part_of(windows[kind], tap, first, CHUNK),
        conv_ref,
        vector_buf,
        value_buf,
    )
    recall(
        lambda row: load(row).wait(),
        lambda row, h: state_buf[row, h * DK : (h + 1) * DK, :],
        vector_buf,
        found_buf,
    )
    finish(
        lambda step, first: part_of(strength_all, step, first, CHUNK),
        lambda step, first: part_of(forget_all, step, first, CHUNK),
        lambda step, first: part_of(gate_all, step, first, CHUNK),
        vector_buf,
        value_buf,
        found_buf,
        normed_buf,
        update_ref,
    )
    flatten_heads(normed_buf, normed_ref)


def send_kernel(wanted_ref, update_ref, tails_ref, state_ref, slots, stored_buf, slot_sem):
    count = slots.shape[0]

    def ship(slot, row):
        return (
            pltpu.make_async_copy(
                stored_buf.at[row], slots.at[slot, pl.ds(0, BODY)], slot_sem.at[0, slot]
            ),
            pltpu.make_async_copy(
                tails_ref.at[row], slots.at[slot, pl.ds(BODY, SLOT - BODY)], slot_sem.at[1, slot]
            ),
        )

    def group(index, carry):
        write_group(index, update_ref, state_ref, stored_buf)

        def begin(slot, carry):
            row = wanted_ref[slot]

            @pl.when((row >= index * GROUP) & (row < (index + 1) * GROUP))
            def _():
                for copy in ship(slot, row):
                    copy.start()

            return carry

        return lax.fori_loop(0, count, begin, carry)

    lax.fori_loop(0, ROWS // GROUP, group, 0)

    def end(slot, carry):
        @pl.when(wanted_ref[slot] >= 0)
        def _():
            for copy in ship(slot, 0):
                copy.wait()

        return carry

    lax.fori_loop(0, count, end, 0)


def second_kernel(
    slot_ref, late_query, late_key, late_value, late_gate, late_strength, late_forget, conv_ref, slots,
    normed_ref, update_ref, last_ref, memory_buf,
    tail_buf, window_query, window_key, window_value,
    vector_buf, value_buf, found_buf, normed_buf, tail_sem, memory_sem,
):
    def load_tail(row):
        return pltpu.make_async_copy(
            slots.at[slot_ref[row], pl.ds(BODY, SLOT - BODY)], tail_buf.at[row], tail_sem.at[row]
        )

    def load(row):
        return pltpu.make_async_copy(
            slots.at[slot_ref[row], pl.ds(0, BODY)], memory_buf.at[row], memory_sem.at[row]
        )

    for row in range(ROWS):
        load_tail(row).start()
    for row in range(ROWS):
        load(row).start()
    wide = widening()
    for row in range(ROWS):
        load_tail(row).wait()
    for row in range(ROWS):
        tails = tail_buf[row]
        last_ref[row] = tails[2 * SLIM :]
        spread = dot(wide, tails)
        for tap in range(TAPS - 1):
            for kind, window in enumerate((window_query, window_key, window_value)):
                start = tap * WIDE + kind * HEADS
                window[(tap * ROWS + row) * HEADS : (tap * ROWS + row + 1) * HEADS, :] = spread[
                    start : start + HEADS
                ]
    windows = (window_query, window_key, window_value)
    fresh = (late_query, late_key, late_value)

    def window(kind, tap, first):
        if tap < TAPS - 1:
            return part_of(windows[kind], tap, first, CHUNK)
        return part_of(fresh[kind], tap - (TAPS - 1), first, CHUNK)

    find_vectors(window, conv_ref, vector_buf, value_buf)
    recall(
        lambda row: load(row).wait(),
        lambda row, h: memory_buf[row, h * DK : (h + 1) * DK, :],
        vector_buf,
        found_buf,
    )
    finish(
        lambda step, first: part_of(late_strength, step, first, CHUNK),
        lambda step, first: part_of(late_forget, step, first, CHUNK),
        lambda step, first: part_of(late_gate, step, first, CHUNK),
        vector_buf,
        value_buf,
        found_buf,
        normed_buf,
        update_ref,
    )
    flatten_heads(normed_buf, normed_ref)


def final_kernel(
    update_ref, last_ref, raw_ref, memory_ref,
    final, query_ref, key_ref, value_ref,
    final_buf, last_buf, final_sem,
):
    def save(row):
        return pltpu.make_async_copy(final_buf.at[row], final.at[row], final_sem.at[row])

    start = 0
    last_buf[...] = last_ref[...].astype(f32).reshape(ROWS * SLIM, DV)
    for ref in (query_ref, key_ref, value_ref):
        width = ref.shape[2]
        for channel in range(width // DV):
            block = last_buf[pl.ds(start // DV + channel, ROWS, stride=SLIM), :]
            ref[0, :, channel * DV : (channel + 1) * DV] = block.astype(bf16)
        for step in range(2):
            ref[1 + step] = raw_ref[step * ROWS : (step + 1) * ROWS, start : start + width]
        start += width

    def group(index, carry):
        write_group(index, update_ref, memory_ref, final_buf)
        for i in range(GROUP):
            save(index * GROUP + i).start()
        return carry

    lax.fori_loop(0, ROWS // GROUP, group, 0)
    for row in range(ROWS):
        save(row).wait()


VMEM = pl.BlockSpec(memory_space=pltpu.VMEM)
SMEM = pl.BlockSpec(memory_space=pltpu.SMEM)
HBM = pl.BlockSpec(memory_space=pltpu.HBM)
PARAMS = pltpu.CompilerParams(vmem_limit_bytes=VMEM_BYTES)


def in_hbm(array):
    return pltpu.with_memory_space_constraint(array, pltpu.HBM)


def shape(dims, kind):
    return jax.ShapeDtypeStruct(dims, kind)


def buffer(array):
    return pltpu.VMEM(array.shape, array.dtype)


def work_buffers():
    return [
        pltpu.VMEM((ROWS, 4 * HEADS, DV), f32),
        pltpu.VMEM((2, ROWS, HEADS, DV), f32),
        pltpu.VMEM((ROWS, 4 * HEADS, DV), f32),
        pltpu.VMEM((2 * ROWS * HEADS, DV), f32),
    ]


def first_half(arrays, state):
    rows = arrays[0].shape[0]
    late = rows // 2
    window = pltpu.VMEM(((TAPS - 1) * ROWS * HEADS + rows * HEADS, DV), f32)
    wide = pltpu.VMEM((rows * HEADS, DV), f32)
    return pl.pallas_call(
        first_kernel,
        in_specs=[HBM] * (len(arrays) + 1),
        out_specs=[VMEM] * 12,
        out_shape=(
            *[shape((late * HEADS, DV), f32)] * 6,
            shape((late, SLIM * DV), bf16),
            shape((ROWS, (TAPS - 1) * SLIM, DV), bf16),
            shape((3, TAPS, HEADS, DV), f32),
            shape((late, HEADS * DV), bf16),
            shape((ROWS, 5 * HEADS, DV), f32),
            shape(state.shape, bf16),
        ),
        scratch_shapes=[
            *[buffer(array) for array in arrays[:-2]],
            *[pltpu.SMEM(array.shape, f32) for array in arrays[-2:]],
            window,
            window,
            window,
            wide,
            wide,
            wide,
            pltpu.VMEM((ROWS * (TAPS - 1) * SLIM, DV), f32),
            *work_buffers(),
            pltpu.SemaphoreType.DMA((12,)),
            pltpu.SemaphoreType.DMA((4 * KEYS,)),
            pltpu.SemaphoreType.DMA((ROWS,)),
        ],
        compiler_params=PARAMS,
        name="first_half",
    )(*[in_hbm(array) for array in arrays], in_hbm(state))


def fill_slots(wanted, update, tails, state):
    return pl.pallas_call(
        send_kernel,
        in_specs=[SMEM] + [VMEM] * 3,
        out_specs=HBM,
        out_shape=shape((wanted.shape[0], SLOT, DV), bf16),
        scratch_shapes=[
            buffer(state),
            pltpu.SemaphoreType.DMA((2, wanted.shape[0])),
        ],
        compiler_params=PARAMS,
        name="fill_slots",
    )(wanted, update, tails, state)


def second_half(slot_of_row, late, conv, slots):
    window = pltpu.VMEM(((TAPS - 1) * ROWS * HEADS, DV), f32)
    return pl.pallas_call(
        second_kernel,
        in_specs=[SMEM] + [VMEM] * 7 + [HBM],
        out_specs=[VMEM] * 4,
        out_shape=(
            shape((2 * ROWS, HEADS * DV), bf16),
            shape((ROWS, 5 * HEADS, DV), f32),
            shape((ROWS, SLIM, DV), bf16),
            shape((ROWS, BODY, DV), bf16),
        ),
        scratch_shapes=[
            pltpu.VMEM((ROWS, SLOT - BODY, DV), bf16),
            window,
            window,
            window,
            *work_buffers(),
            pltpu.SemaphoreType.DMA((ROWS,)),
            pltpu.SemaphoreType.DMA((ROWS,)),
        ],
        compiler_params=PARAMS,
        name="second_half",
    )(slot_of_row, *late, conv, in_hbm(slots))


def last_memory(update, last, raw, memory):
    return pl.pallas_call(
        final_kernel,
        in_specs=[VMEM] * 4,
        out_specs=[HBM] + [VMEM] * 3,
        out_shape=(
            shape((ROWS, BODY, DV), bf16),
            shape((TAPS - 1, ROWS, KEYS * DK), bf16),
            shape((TAPS - 1, ROWS, KEYS * DK), bf16),
            shape((TAPS - 1, ROWS, HEADS * DV), bf16),
        ),
        scratch_shapes=[
            buffer(memory),
            pltpu.VMEM((ROWS * SLIM, DV), f32),
            pltpu.SemaphoreType.DMA((ROWS,)),
        ],
        compiler_params=PARAMS,
        name="last_memory",
    )(update, last, raw, memory)


def sum_heads(partial):
    count, me = lax.axis_size("tensor"), lax.axis_index("tensor")
    width = partial.shape[1] // count

    def block(shift):
        return lax.dynamic_slice_in_dim(partial, (me + shift) % count * width, width, axis=1)

    total = block(0)
    for shift in range(1, count):
        pairs = [(i, (i + shift) % count) for i in range(count)]
        total = total + lax.ppermute(block(shift), "tensor", pairs)
    return total.astype(bf16)


def per_device(
    inputs,
    w_query,
    w_key,
    w_value,
    w_gate_z,
    w_beta,
    w_decay,
    conv_query,
    conv_key,
    conv_value,
    decay_log,
    dt_bias,
    norm_gain,
    w_out,
    state,
    tail_query,
    tail_key,
    tail_value,
    parents,
):
    groups = lax.axis_size("branch")
    source, offset = parents // ROWS, parents % ROWS
    hits = source[:, None] == jnp.arange(groups, dtype=jnp.int32)[None, :]
    wanted = jnp.sum(jnp.where(hits, offset[:, None] + 1, 0), axis=0) - 1
    requested = lax.all_to_all(
        wanted.reshape(groups, 1), "branch", split_axis=0, concat_axis=0, tiled=True
    ).reshape(groups)

    flat_state = state.reshape(ROWS, BODY, DV)
    *late, raw, stored_tails, conv, normed, update, held = first_half(
        (
            inputs.reshape(-1, inputs.shape[-1]),
            norm_gain[None],
            tail_query.transpose(1, 0, 2),
            tail_key.transpose(1, 0, 2),
            tail_value.transpose(1, 0, 2),
            conv_query,
            conv_key,
            conv_value,
            w_query,
            w_key,
            w_value,
            w_gate_z,
            w_beta.T,
            w_decay.T,
            decay_log,
            dt_bias,
        ),
        flat_state,
    )
    shipped = fill_slots(requested, update, stored_tails, held)
    arrived = lax.all_to_all(shipped, "branch", split_axis=0, concat_axis=0, tiled=True)

    first_rows = sum_heads(dot(normed, w_out))

    normed, update, last, memory = second_half(source, late, conv, arrived)
    second_rows = sum_heads(dot(normed, w_out))
    final_state, *final_tails = last_memory(update, last, raw, memory)

    out_rows = jnp.concatenate([first_rows, second_rows], axis=0)
    out_rows = out_rows.reshape(inputs.shape[0], ROWS, -1)
    return (
        out_rows,
        final_state.reshape(state.shape),
        *[tail.transpose(1, 0, 2) for tail in final_tails],
    )


def solution(mesh):
    return jax.shard_map(
        per_device,
        mesh=mesh,
        in_specs=(
            P(None, "branch", None),
            P(None, "tensor"),
            P(None, "tensor"),
            P(None, "tensor"),
            P(None, "tensor"),
            P(None, "tensor"),
            P(None, "tensor"),
            P(None, "tensor"),
            P(None, "tensor"),
            P(None, "tensor"),
            P("tensor"),
            P("tensor"),
            P(),
            P("tensor", None),
            P("branch", "tensor", None, None),
            P("branch", None, "tensor"),
            P("branch", None, "tensor"),
            P("branch", None, "tensor"),
            P("branch"),
        ),
        out_specs=(
            P(None, "branch", "tensor"),
            P("branch", "tensor", None, None),
            P("branch", None, "tensor"),
            P("branch", None, "tensor"),
            P("branch", None, "tensor"),
        ),
        check_vma=False,
    )
```

profile of v0, /device:TPU:0, one launch (start us, length us, event | category | flops | bytes accessed | tf_op | source)
XLA Modules:
  0.0 163.2 jit_solution(6597264185390844171)
XLA Ops:
  0.6 0.7 fusion
  1.3 0.1 select_reduce_fusion
  1.4 0.7 copy.26
  2.1 8.2 %all-to-all-start = ((s32[32,1,1]{2,1,0:T(1,128)}), s32[32,1,1]{2,1,0:T(1,128)S(1)}, u32[]{:S(2)}, u32[]{:S(2)}) async-start(s32[32,1,1]{2,1,0:T(1,128)} %copy.26), calls=%async_computation | async-start | bytes 32768 | tf_op jit(solution)/shard_map/all_to_all | solution.py:633
  10.3 8.5 %first_half.1 = (f32[256,128]{1,0:T(8,128)S(1)}, f32[256,128]{1,0:T(8,128)S(1)}, f32[256,128]{1,0:T(8,128)S(1)}, f32[256,128]{1,0:T(8,128)S(1)}, f32[256,128]{1,...) custom-call(bf16[64,2048]{1,0:T(8,128)(2,1)} %bitcast.20, ...), custom_call_target="tpu_custom_call" | custom-call | tf_op jit(solution)/shard_map/first_half/pallas_call | solution.py:499
  18.9 0.0 copy-start
  18.9 2.0 %copy-done = bf16[16,1024,128]{2,1,0:T(8,128)(2,1)} copy-done((bf16[16,1024,128]{2,1,0:T(8,128)(2,1)}, bf16[16,1024,128]{2,1,0:T(8,128)(2,1)S(1)}, u32[]{:S(2)}) %copy-start) | copy-done | bytes 4194328
  20.9 0.0 all-to-all-done
  20.9 0.7 reduce.wanted_ref
  21.6 0.0 copy-start.1
  21.6 2.2 %copy-done.1 = bf16[16,1024,128]{2,1,0:T(8,128)(2,1)S(1)} copy-done((bf16[16,1024,128]{2,1,0:T(8,128)(2,1)S(1)}, bf16[16,1024,128]{2,1,0:T(8,128)(2,1)}, u32[]{:S(2)}) %copy-start.1) | copy-done | bytes 4194328
  23.8 5.0 %fill_slots.1 = bf16[32,1072,128]{2,1,0:T(8,128)(2,1)} custom-call(s32[32]{0:T(128)S(1)} %reduce.wanted_ref, f32[16,40,128]{2,1,0:T(8,128)S(1)} %get-tuple-element.33.update_ref, bf16[16,48,128]{2,1,0:T(8,128)(2,1)S(1)} %get-tuple-element.34.tails_ref, bf16[16,1024,128]{2,1,0:T(8,128)(2,1)S(1)} %copy-done.1), custom_call_target="tpu_custom_call" | custom-call | tf_op jit(solution)/shard_map/fill_slots/pallas_call | solution.py:533
  28.8 7.8 %all-to-all-start.1 = ((bf16[32,1072,128]{2,1,0:T(8,128)(2,1)}), bf16[32,1072,128]{2,1,0:T(8,128)(2,1)}, u32[]{:S(2)}, u32[]{:S(2)}) async-start(bf16[32,1072,128]{2,1,0:T(8,128)(2,1)} %fill_slots.1), calls=%async_computation.1 | async-start | bytes 17563648 | tf_op jit(solution)/shard_map/all_to_all | solution.py:660
  36.6 3.0 %fusion.1 = f32[32,2048]{1,0:T(8,128)S(1)} fusion(bf16[32,1024]{1,0:T(8,128)(2,1)S(1)} %get-tuple-element.25, bf16[1024,2048]{1,0:T(8,128)(2,1)} %param.32), kind=kOutput, calls=%fused_computation.18 | convolution fusion | flops 134217728 | bytes 4521984 | tf_op jit(solution)/shard_map/dot_general | solution.py:31
  39.6 1.6 %collective-permute-start = (f32[32,512]{1,0:T(8,128)S(1)}, f32[32,512]{1,0:T(8,128)S(1)}, u32[]{:S(2)}, u32[]{:S(2)}) collective-permute-start(f32[32,512]{1,0:T(8,128)S(1)} %get-tuple-element.45), channel_id=1, source_target_pairs={{0,1},{1,2},{2,3},{3,0},{4,5},{5,6},{6,7},{7,4},{8,9},{9,10},{10,1... | collective-permute-start | bytes 196616 | tf_op jit(solution)/shard_map/ppermute | solution.py:604
  41.3 1.7 %collective-permute-start.2 = (f32[32,512]{1,0:T(8,128)S(1)}, f32[32,512]{1,0:T(8,128)S(1)}, u32[]{:S(2)}, u32[]{:S(2)}) collective-permute-start(f32[32,512]{1,0:T(8,128)S(1)} %get-tuple-element.46), channel_id=1, source_target_pairs={{0,3},{1,0},{2,1},{3,2},{4,7},{5,4},{6,5},{7,6},{8,11},{9,8},{10,9... | collective-permute-start | bytes 196616 | tf_op jit(solution)/shard_map/ppermute | solution.py:604
  42.9 2.0 %collective-permute-start.1 = (f32[32,512]{1,0:T(8,128)S(1)}, f32[32,512]{1,0:T(8,128)S(1)}, u32[]{:S(2)}, u32[]{:S(2)}) collective-permute-start(f32[32,512]{1,0:T(8,128)S(1)} %get-tuple-element.47), channel_id=1, source_target_pairs={{0,2},{1,3},{2,0},{3,1},{4,6},{5,7},{6,4},{7,5},{8,10},{9,11},{10,... | collective-permute-start | bytes 196616 | tf_op jit(solution)/shard_map/ppermute | solution.py:604
  44.9 102.6 %all-to-all-done.1.slots = bf16[32,1072,128]{2,1,0:T(8,128)(2,1)} async-done(((bf16[32,1072,128]{2,1,0:T(8,128)(2,1)}), bf16[32,1072,128]{2,1,0:T(8,128)(2,1)}, u32[]{:S(2)}, u32[]{:S(2)}) %all-to-all-start.1) | async-done | bytes 8781856 | tf_op jit(solution)/shard_map/all_to_all | solution.py:660
  147.5 0.0 copy-start.2
  147.5 5.0 %second_half.1 = (bf16[32,1024]{1,0:T(8,128)(2,1)S(1)}, f32[16,40,128]{2,1,0:T(8,128)S(1)}, bf16[16,16,128]{2,1,0:T(8,128)(2,1)S(1)}, bf16[16,1024,128]{2,1,0:T(8,128)(2,1)S(1)}) custom-call(s32[16]{0:T(128)S(1)} %get-tuple-element.52.slot_ref, f32[256,128]{1,0:T(8,128)S(1)} %get-tuple-element.26.late_query, f32[256,128]{1,0:T(8,128)S(1)} %get-tuple-element.27.late_key, ...), custom_call_target="tpu_custom_call" | custom-call | tf_op jit(solution)/shard_map/second_half/pallas_call | solution.py:549
  152.5 0.0 copy-done.2
  152.5 0.8 fusion.2
  153.4 1.6 %collective-permute-start.3 = (f32[32,512]{1,0:T(8,128)S(1)}, f32[32,512]{1,0:T(8,128)S(1)}, u32[]{:S(2)}, u32[]{:S(2)}) collective-permute-start(f32[32,512]{1,0:T(8,128)S(1)} %get-tuple-element.48), channel_id=1, source_target_pairs={{0,1},{1,2},{2,3},{3,0},{4,5},{5,6},{6,7},{7,4},{8,9},{9,10},{10,1... | collective-permute-start | bytes 196616 | tf_op jit(solution)/shard_map/ppermute | solution.py:604
  155.0 1.7 %collective-permute-start.5 = (f32[32,512]{1,0:T(8,128)S(1)}, f32[32,512]{1,0:T(8,128)S(1)}, u32[]{:S(2)}, u32[]{:S(2)}) collective-permute-start(f32[32,512]{1,0:T(8,128)S(1)} %get-tuple-element.49), channel_id=1, source_target_pairs={{0,3},{1,0},{2,1},{3,2},{4,7},{5,4},{6,5},{7,6},{8,11},{9,8},{10,9... | collective-permute-start | bytes 196616 | tf_op jit(solution)/shard_map/ppermute | solution.py:604
  156.7 0.0 collective-permute-done
  156.7 2.0 %collective-permute-start.4 = (f32[32,512]{1,0:T(8,128)S(1)}, f32[32,512]{1,0:T(8,128)S(1)}, u32[]{:S(2)}, u32[]{:S(2)}) collective-permute-start(f32[32,512]{1,0:T(8,128)S(1)} %get-tuple-element.50), channel_id=1, source_target_pairs={{0,2},{1,3},{2,0},{3,1},{4,6},{5,7},{6,4},{7,5},{8,10},{9,11},{10,... | collective-permute-start | bytes 196616 | tf_op jit(solution)/shard_map/ppermute | solution.py:604
  158.6 0.0 collective-permute-done.2
  158.7 0.0 collective-permute-done.1
  158.7 3.8 %last_memory.1 = (bf16[16,1024,128]{2,1,0:T(8,128)(2,1)}, bf16[3,16,512]{2,1,0:T(8,128)(2,1)}, bf16[3,16,512]{2,1,0:T(8,128)(2,1)}, bf16[3,16,1024]{2,1,0:T(8,128)(2,1)}) custom-call(f32[16,40,128]{2,1,0:T(8,128)S(1)} %get-tuple-element.37.update_ref, bf16[16,16,128]{2,1,0:T(8,128)(2,1)S(1)} %get-tuple-element.38.last_ref, ...), custom_call_target="tpu_custom_call" | custom-call | tf_op jit(solution)/shard_map/last_memory/pallas_call | solution.py:574
  162.5 0.0 collective-permute-done.3
  162.5 0.0 collective-permute-done.5
  162.5 0.0 collective-permute-done.4
  162.5 0.6 pad_maximum_fusion
  (5 shorter events, 0.1 us)
Async XLA Ops:
  2.1 18.8 %all-to-all-start = ((s32[32,1,1]{2,1,0:T(1,128)}), s32[32,1,1]{2,1,0:T(1,128)S(1)}, u32[]{:S(2)}, u32[]{:S(2)}) async-start(s32[32,1,1]{2,1,0:T(1,128)} %copy.26), calls=%async_computation | async-start | bytes 32768 | tf_op jit(solution)/shard_map/all_to_all | solution.py:633
  18.9 2.0 %copy-start = (bf16[16,1024,128]{2,1,0:T(8,128)(2,1)}, bf16[16,1024,128]{2,1,0:T(8,128)(2,1)S(1)}, u32[]{:S(2)}) copy-start(bf16[16,1024,128]{2,1,0:T(8,128)(2,1)S(1)} %get-tuple-element.35.state_ref) | copy-start | bytes 12582916
  21.6 2.2 %copy-start.1 = (bf16[16,1024,128]{2,1,0:T(8,128)(2,1)S(1)}, bf16[16,1024,128]{2,1,0:T(8,128)(2,1)}, u32[]{:S(2)}) copy-start(bf16[16,1024,128]{2,1,0:T(8,128)(2,1)} %copy-done) | copy-start | bytes 12582916
  28.8 118.7 %all-to-all-start.1 = ((bf16[32,1072,128]{2,1,0:T(8,128)(2,1)}), bf16[32,1072,128]{2,1,0:T(8,128)(2,1)}, u32[]{:S(2)}, u32[]{:S(2)}) async-start(bf16[32,1072,128]{2,1,0:T(8,128)(2,1)} %fill_slots.1), calls=%async_computation.1 | async-start | bytes 17563648 | tf_op jit(solution)/shard_map/all_to_all | solution.py:660
  39.6 117.0 %collective-permute-start = (f32[32,512]{1,0:T(8,128)S(1)}, f32[32,512]{1,0:T(8,128)S(1)}, u32[]{:S(2)}, u32[]{:S(2)}) collective-permute-start(f32[32,512]{1,0:T(8,128)S(1)} %get-tuple-element.45), channel_id=1, source_target_pairs={{0,1},{1,2},{2,3},{3,0},{4,5},{5,6},{6,7},{7,4},{8,9},{9,10},{10,1... | collective-permute-start | bytes 196616 | tf_op jit(solution)/shard_map/ppermute | solution.py:604
  41.3 117.4 %collective-permute-start.2 = (f32[32,512]{1,0:T(8,128)S(1)}, f32[32,512]{1,0:T(8,128)S(1)}, u32[]{:S(2)}, u32[]{:S(2)}) collective-permute-start(f32[32,512]{1,0:T(8,128)S(1)} %get-tuple-element.46), channel_id=1, source_target_pairs={{0,3},{1,0},{2,1},{3,2},{4,7},{5,4},{6,5},{7,6},{8,11},{9,8},{10,9... | collective-permute-start | bytes 196616 | tf_op jit(solution)/shard_map/ppermute | solution.py:604
  42.9 115.7 %collective-permute-start.1 = (f32[32,512]{1,0:T(8,128)S(1)}, f32[32,512]{1,0:T(8,128)S(1)}, u32[]{:S(2)}, u32[]{:S(2)}) collective-permute-start(f32[32,512]{1,0:T(8,128)S(1)} %get-tuple-element.47), channel_id=1, source_target_pairs={{0,2},{1,3},{2,0},{3,1},{4,6},{5,7},{6,4},{7,5},{8,10},{9,11},{10,... | collective-permute-start | bytes 196616 | tf_op jit(solution)/shard_map/ppermute | solution.py:604
  147.5 5.0 %copy-start.2 = (bf16[1024,2048]{1,0:T(8,128)(2,1)S(1)}, bf16[1024,2048]{1,0:T(8,128)(2,1)}, u32[]{:S(2)}) copy-start(bf16[1024,2048]{1,0:T(8,128)(2,1)} %param.32) | copy-start | bytes 12582916
  153.4 9.1 %collective-permute-start.3 = (f32[32,512]{1,0:T(8,128)S(1)}, f32[32,512]{1,0:T(8,128)S(1)}, u32[]{:S(2)}, u32[]{:S(2)}) collective-permute-start(f32[32,512]{1,0:T(8,128)S(1)} %get-tuple-element.48), channel_id=1, source_target_pairs={{0,1},{1,2},{2,3},{3,0},{4,5},{5,6},{6,7},{7,4},{8,9},{9,10},{10,1... | collective-permute-start | bytes 196616 | tf_op jit(solution)/shard_map/ppermute | solution.py:604
  155.0 7.5 %collective-permute-start.5 = (f32[32,512]{1,0:T(8,128)S(1)}, f32[32,512]{1,0:T(8,128)S(1)}, u32[]{:S(2)}, u32[]{:S(2)}) collective-permute-start(f32[32,512]{1,0:T(8,128)S(1)} %get-tuple-element.49), channel_id=1, source_target_pairs={{0,3},{1,0},{2,1},{3,2},{4,7},{5,4},{6,5},{7,6},{8,11},{9,8},{10,9... | collective-permute-start | bytes 196616 | tf_op jit(solution)/shard_map/ppermute | solution.py:604
  156.7 5.8 %collective-permute-start.4 = (f32[32,512]{1,0:T(8,128)S(1)}, f32[32,512]{1,0:T(8,128)S(1)}, u32[]{:S(2)}, u32[]{:S(2)}) collective-permute-start(f32[32,512]{1,0:T(8,128)S(1)} %get-tuple-element.50), channel_id=1, source_target_pairs={{0,2},{1,3},{2,0},{3,1},{4,6},{5,7},{6,4},{7,5},{8,10},{9,11},{10,... | collective-permute-start | bytes 196616 | tf_op jit(solution)/shard_map/ppermute | solution.py:604
where the time goes:
time: 163 us
  waiting for transfers between devices  103 us (63%)
  starting transfers between devices  26.6 us (16%)
  Pallas kernels  22.3 us (14%)
  local copies, waits for them, and re-layouts  4.94 us (3%)
  matrix products  3.84 us (2%)
  other arithmetic  2.1 us (1%)
    all_to_all x1, waiting for transfers between devices, per_device(): lax.all_to_all(shipped, 'branch', split_axis=0, concat_axis=0, tiled=True)  103 us
    ppermute x6, starting transfers between devices, sum_heads(): total = total + lax.ppermute(block(shift), 'tensor', pairs)  10.6 us
    pallas_call x1, Pallas kernels, first_half(): pl.pallas_call(first_kernel, in_specs=[HBM] * (len(arrays) + 1), out_spec...  8.54 us
    all_to_all x1, starting transfers between devices, per_device(): lax.all_to_all(wanted.reshape(groups, 1), 'branch', split_axis=0, concat_...  8.25 us
    all_to_all x1, starting transfers between devices, per_device(): lax.all_to_all(shipped, 'branch', split_axis=0, concat_axis=0, tiled=True)  7.75 us
    pallas_call x1, Pallas kernels, fill_slots(): pl.pallas_call(send_kernel, in_specs=[SMEM] + [VMEM] * 3, out_specs=HBM,...  5 us
    pallas_call x1, Pallas kernels, second_half(): pl.pallas_call(second_kernel, in_specs=[SMEM] + [VMEM] * 7 + [HBM], out_s...  4.98 us
    unnamed x6, local copies, waits for them, and re-layouts  4.2 us
  transfers between devices with their start and end apart: 8, of which 1 were waited for; matrix products, arithmetic and copies ran while one was open for 2% of the time, Pallas kernels for 11%

commit v1 on v0

--- a/solution.py
+++ b/solution.py
@@ -17,6 +17,7 @@
 SLOT = BODY + (TAPS - 1) * SLIM
 VMEM_BYTES = 48 * 1024 * 1024
 CHUNK = 4
+PARTS = 4
 GROUP = 4
 f32 = jnp.float32
 bf16 = jnp.bfloat16
@@ -163,10 +164,10 @@
     x, gain, tail_query, tail_key, tail_value, conv_query, conv_key, conv_value,
     w_query, w_key, w_value, w_gate, w_beta, w_decay, decay_log, dt_bias, state,
     late_query_ref, late_key_ref, late_value_ref, late_gate_ref, late_strength_ref, late_forget_ref,
-    raw_ref, stored_ref, conv_ref, normed_ref, update_ref, state_buf,
+    raw_ref, stored_ref, conv_ref, normed_ref, update_ref,
     x_buf, gain_buf, tail_query_buf, tail_key_buf, tail_value_buf,
     conv_query_buf, conv_key_buf, conv_value_buf,
-    query_buf, key_buf, value_weight_buf, gate_weight_buf, beta_buf, decay_buf, decay_ref, bias_ref,
+    query_buf, key_buf, value_weight_buf, gate_weight_buf, beta_buf, decay_buf, decay_ref, bias_ref, state_buf,
     window_query, window_key, window_value, gate_all, strength_all, forget_all, stored_buf,
     vector_buf, value_buf, found_buf, normed_buf,
     small_sem, weight_sem, state_sem,
@@ -332,8 +333,16 @@
     flatten_heads(normed_buf, normed_ref)
 
 
-def send_kernel(wanted_ref, update_ref, tails_ref, state_ref, slots, stored_buf, slot_sem):
+def send_kernel(
+    wanted_ref, update_ref, tails_ref, state, slots, state_buf, stored_buf, state_sem, slot_sem
+):
     count = slots.shape[0]
+
+    def load(row):
+        return pltpu.make_async_copy(state.at[row], state_buf.at[row], state_sem.at[row])
+
+    for row in range(ROWS):
+        load(row).start()
 
     def ship(slot, row):
         return (
@@ -346,10 +355,12 @@
         )
 
     def group(index, carry):
-        write_group(index, update_ref, state_ref, stored_buf)
+        for i in range(GROUP):
+            load(index * GROUP + i).wait()
+        write_group(index, update_ref, state_buf, stored_buf)
 
         def begin(slot, carry):
-            row = wanted_ref[slot]
+            row = wanted_ref[slot, 0, 0]
 
             @pl.when((row >= index * GROUP) & (row < (index + 1) * GROUP))
             def _():
@@ -363,7 +374,7 @@
     lax.fori_loop(0, ROWS // GROUP, group, 0)
 
     def end(slot, carry):
-        @pl.when(wanted_ref[slot] >= 0)
+        @pl.when(wanted_ref[slot, 0, 0] >= 0)
         def _():
             for copy in ship(slot, 0):
                 copy.wait()
@@ -374,11 +385,16 @@
 
 
 def second_kernel(
-    slot_ref, late_query, late_key, late_value, late_gate, late_strength, late_forget, conv_ref, slots,
-    normed_ref, update_ref, last_ref, memory_buf,
-    tail_buf, window_query, window_key, window_value,
-    vector_buf, value_buf, found_buf, normed_buf, tail_sem, memory_sem,
+    slot_ref, late_query, late_key, late_value, late_gate, late_strength, late_forget, conv_ref, early_ref, slots, w_out,
+    *refs,
 ):
+    sums = refs[:PARTS]
+    (
+        update_ref, last_ref, memory_buf,
+        tail_buf, window_query, window_key, window_value,
+        vector_buf, value_buf, found_buf, normed_buf, out_buf, normed_ref,
+        tail_sem, memory_sem, out_sem,
+    ) = refs[PARTS:]
     def load_tail(row):
         return pltpu.make_async_copy(
             slots.at[slot_ref[row], pl.ds(BODY, SLOT - BODY)], tail_buf.at[row], tail_sem.at[row]
@@ -393,6 +409,17 @@
         load_tail(row).start()
     for row in range(ROWS):
         load(row).start()
+    width = out_buf.shape[2]
+    place = lax.axis_index("tensor")
+
+    def load_out(shift):
+        start = pl.multiple_of((place + shift) % PARTS * width, width)
+        return pltpu.make_async_copy(
+            w_out.at[:, pl.ds(start, width)], out_buf.at[shift], out_sem.at[shift]
+        )
+
+    for shift in range(PARTS):
+        load_out(shift).start()
     wide = widening()
     for row in range(ROWS):
         load_tail(row).wait()
@@ -431,7 +458,13 @@
         normed_buf,
         update_ref,
     )
-    flatten_heads(normed_buf, normed_ref)
+    normed_ref[: 2 * ROWS, :] = early_ref[...]
+    flatten_heads(normed_buf, normed_ref.at[2 * ROWS :])
+    for shift in range(PARTS):
+        load_out(shift).wait()
+    normed = normed_ref[...]
+    for shift in range(PARTS):
+        sums[shift][...] = dot(normed, out_buf[shift])
 
 
 def final_kernel(
@@ -499,7 +532,7 @@
     return pl.pallas_call(
         first_kernel,
         in_specs=[HBM] * (len(arrays) + 1),
-        out_specs=[VMEM] * 12,
+        out_specs=[VMEM] * 11,
         out_shape=(
             *[shape((late * HEADS, DV), f32)] * 6,
             shape((late, SLIM * DV), bf16),
@@ -507,11 +540,11 @@
             shape((3, TAPS, HEADS, DV), f32),
             shape((late, HEADS * DV), bf16),
             shape((ROWS, 5 * HEADS, DV), f32),
-            shape(state.shape, bf16),
         ),
         scratch_shapes=[
             *[buffer(array) for array in arrays[:-2]],
             *[pltpu.SMEM(array.shape, f32) for array in arrays[-2:]],
+            buffer(state),
             window,
             window,
             window,
@@ -532,26 +565,29 @@
 def fill_slots(wanted, update, tails, state):
     return pl.pallas_call(
         send_kernel,
-        in_specs=[SMEM] + [VMEM] * 3,
+        in_specs=[SMEM, VMEM, VMEM, HBM],
         out_specs=HBM,
         out_shape=shape((wanted.shape[0], SLOT, DV), bf16),
         scratch_shapes=[
             buffer(state),
+            buffer(state),
+            pltpu.SemaphoreType.DMA((ROWS,)),
             pltpu.SemaphoreType.DMA((2, wanted.shape[0])),
         ],
         compiler_params=PARAMS,
         name="fill_slots",
-    )(wanted, update, tails, state)
-
-
-def second_half(slot_of_row, late, conv, slots):
+    )(wanted, update, tails, in_hbm(state))
+
+
+def second_half(slot_of_row, late, conv, normed, slots, w_out):
     window = pltpu.VMEM(((TAPS - 1) * ROWS * HEADS, DV), f32)
-    return pl.pallas_call(
+    rows, width = 2 * normed.shape[0], w_out.shape[1] // PARTS
+    *sums, update, last, memory = pl.pallas_call(
         second_kernel,
-        in_specs=[SMEM] + [VMEM] * 7 + [HBM],
-        out_specs=[VMEM] * 4,
+        in_specs=[SMEM] + [VMEM] * 8 + [HBM] * 2,
+        out_specs=[VMEM] * (PARTS + 3),
         out_shape=(
-            shape((2 * ROWS, HEADS * DV), bf16),
+            *[shape((rows, width), f32)] * PARTS,
             shape((ROWS, 5 * HEADS, DV), f32),
             shape((ROWS, SLIM, DV), bf16),
             shape((ROWS, BODY, DV), bf16),
@@ -562,12 +598,16 @@
             window,
             window,
             *work_buffers(),
+            pltpu.VMEM((PARTS, w_out.shape[0], width), bf16),
+            pltpu.VMEM((rows, normed.shape[1]), bf16),
             pltpu.SemaphoreType.DMA((ROWS,)),
             pltpu.SemaphoreType.DMA((ROWS,)),
+            pltpu.SemaphoreType.DMA((PARTS,)),
         ],
         compiler_params=PARAMS,
         name="second_half",
-    )(slot_of_row, *late, conv, in_hbm(slots))
+    )(slot_of_row, *late, conv, normed, in_hbm(slots), in_hbm(w_out))
+    return sums, update, last, memory
 
 
 def last_memory(update, last, raw, memory):
@@ -591,17 +631,11 @@
     )(update, last, raw, memory)
 
 
-def sum_heads(partial):
-    count, me = lax.axis_size("tensor"), lax.axis_index("tensor")
-    width = partial.shape[1] // count
-
-    def block(shift):
-        return lax.dynamic_slice_in_dim(partial, (me + shift) % count * width, width, axis=1)
-
-    total = block(0)
-    for shift in range(1, count):
-        pairs = [(i, (i + shift) % count) for i in range(count)]
-        total = total + lax.ppermute(block(shift), "tensor", pairs)
+def sum_heads(blocks):
+    total = blocks[0]
+    for shift in range(1, PARTS):
+        pairs = [(i, (i + shift) % PARTS) for i in range(PARTS)]
+        total = total + lax.ppermute(blocks[shift], "tensor", pairs)
     return total.astype(bf16)
 
 
@@ -631,11 +665,11 @@
     hits = source[:, None] == jnp.arange(groups, dtype=jnp.int32)[None, :]
     wanted = jnp.sum(jnp.where(hits, offset[:, None] + 1, 0), axis=0) - 1
     requested = lax.all_to_all(
-        wanted.reshape(groups, 1), "branch", split_axis=0, concat_axis=0, tiled=True
-    ).reshape(groups)
+        wanted.reshape(groups, 1, 1), "branch", split_axis=0, concat_axis=0, tiled=True
+    )
 
     flat_state = state.reshape(ROWS, BODY, DV)
-    *late, raw, stored_tails, conv, normed, update, held = first_half(
+    *late, raw, stored_tails, conv, normed, update = first_half(
         (
             inputs.reshape(-1, inputs.shape[-1]),
             norm_gain[None],
@@ -656,17 +690,12 @@
         ),
         flat_state,
     )
-    shipped = fill_slots(requested, update, stored_tails, held)
+    shipped = fill_slots(requested, update, stored_tails, flat_state)
     arrived = lax.all_to_all(shipped, "branch", split_axis=0, concat_axis=0, tiled=True)
 
-    first_rows = sum_heads(dot(normed, w_out))
-
-    normed, update, last, memory = second_half(source, late, conv, arrived)
-    second_rows = sum_heads(dot(normed, w_out))
+    sums, update, last, memory = second_half(source, late, conv, normed, arrived, w_out)
+    out_rows = sum_heads(sums).reshape(inputs.shape[0], ROWS, -1)
     final_state, *final_tails = last_memory(update, last, raw, memory)
-
-    out_rows = jnp.concatenate([first_rows, second_rows], axis=0)
-    out_rows = out_rows.reshape(inputs.shape[0], ROWS, -1)
     return (
         out_rows,
         final_state.reshape(state.shape),

time: 163 us -> 152 us (0.933)
  blocking collectives: 0 us -> 108 us
  waiting for transfers between devices: 103 us -> 1.26 us
  starting transfers between devices: 26.6 us -> 14.1 us
  local copies, waits for them, and re-layouts: 4.94 us -> 0.69 us
  matrix products: 3.84 us -> 0 us
  Pallas kernels: 22.3 us -> 25.7 us
    all_to_all x0 -> x1, blocking collectives: none -> 108 us  [per_device(): lax.all_to_all(shipped, 'branch', split_axis=0, concat_axis=0, tiled=True)]
    all_to_all x2 -> x1, waiting for transfers between devices: 103 us -> 0.01 us  [per_device(): lax.all_to_all(wanted.reshape(groups, 1, 1), 'branch', split_axis=0, conc...]
    all_to_all x2 -> x1, starting transfers between devices: 16 us -> 8.24 us  [per_device(): lax.all_to_all(wanted.reshape(groups, 1, 1), 'branch', split_axis=0, conc...]
    ppermute x6 -> x3, starting transfers between devices: 10.6 us -> 5.89 us  [sum_heads(): total = total + lax.ppermute(blocks[shift], 'tensor', pairs)]
    unnamed x6 -> x0, local copies, waits for them, and re-layouts: 4.2 us -> none
    dot_general x2 -> x0, matrix products: 3.84 us -> none  [dot(): return jnp.dot(left, right, preferred_element_type=f32)]
    pallas_call x2, Pallas kernels: 9.97 us -> 13.4 us  [the longest x1 6.89 us: fill_slots(): pl.pallas_call(send_kernel, in_specs=[SMEM, VMEM, VMEM, HBM], out_specs=H...]
  transfers between devices with their start and end apart: 8 -> 4, of which waited for: 1 -> 1; matrix products, arithmetic and copies ran while one was open for 2% -> 0% of each run, Pallas kernels for 11% -> 8%
where the time goes in v1:
time: 152 us; the launch traced here: 151 us
  blocking collectives  108 us (71%)
  Pallas kernels  25.7 us (17%)
  starting transfers between devices  14.1 us (9%)
    all_to_all x1, blocking collectives, per_device(): lax.all_to_all(shipped, 'branch', split_axis=0, concat_axis=0, tiled=True)  108 us
    pallas_call x1, Pallas kernels, first_half(): pl.pallas_call(first_kernel, in_specs=[HBM] * (len(arrays) + 1), out_spec...  8.53 us
    all_to_all x1, starting transfers between devices, per_device(): lax.all_to_all(wanted.reshape(groups, 1, 1), 'branch', split_axis=0, conc...  8.24 us
    pallas_call x1, Pallas kernels, fill_slots(): pl.pallas_call(send_kernel, in_specs=[SMEM, VMEM, VMEM, HBM], out_specs=H...  6.89 us
    pallas_call x1, Pallas kernels, second_half(): pl.pallas_call(second_kernel, in_specs=[SMEM] + [VMEM] * 8 + [HBM] * 2, o...  6.51 us
    ppermute x3, starting transfers between devices, sum_heads(): total = total + lax.ppermute(blocks[shift], 'tensor', pairs)  5.89 us
    pallas_call x1, Pallas kernels, last_memory(): pl.pallas_call(final_kernel, in_specs=[VMEM] * 4, out_specs=[HBM] + [VMEM...  3.78 us
  transfers between devices with their start and end apart: 4, of which 1 were waited for; matrix products, arithmetic and copies ran while one was open for 0% of the time, Pallas kernels for 8%

profile of v1, /device:TPU:0, one launch (start us, length us, event | category | flops | bytes accessed | tf_op | source)
XLA Modules:
  0.0 151.5 jit_solution(9747433482008393620)
XLA Ops:
  0.6 0.7 fusion
  1.3 0.1 select_reduce_fusion
  1.4 0.7 copy.25
  2.1 8.2 %all-to-all-start = ((s32[32,1,1]{2,1,0:T(1,128)}), s32[32,1,1]{2,1,0:T(1,128)S(1)}, u32[]{:S(2)}, u32[]{:S(2)}) async-start(s32[32,1,1]{2,1,0:T(1,128)} %copy.25), calls=%async_computation | async-start | bytes 32768 | tf_op jit(solution)/shard_map/all_to_all | solution.py:667
  10.3 8.5 %first_half.1 = (f32[256,128]{1,0:T(8,128)S(1)}, f32[256,128]{1,0:T(8,128)S(1)}, f32[256,128]{1,0:T(8,128)S(1)}, f32[256,128]{1,0:T(8,128)S(1)}, f32[256,128]{1,...) custom-call(bf16[64,2048]{1,0:T(8,128)(2,1)} %bitcast.17, ...), custom_call_target="tpu_custom_call" | custom-call | tf_op jit(solution)/shard_map/first_half/pallas_call | solution.py:532
  18.9 0.0 all-to-all-done.wanted_ref
  18.9 6.9 %fill_slots.1 = bf16[32,1072,128]{2,1,0:T(8,128)(2,1)} custom-call(s32[32,1,1]{2,1,0:T(1,128)S(1)} %all-to-all-done.wanted_ref, f32[16,40,128]{2,1,0:T(8,128)S(1)} %get-tuple-element.35.update_ref, bf16[16,48,128]{2,1,0:T(8,128)(2,1)S(1)} %get-tuple-element.36.tails_ref, bf16[16,1024,128]{2,1,0:T(8,128)(2,1)} %bitcast.16), custom_call_target="tpu_custom_call" | custom-call | tf_op jit(solution)/shard_map/fill_slots/pallas_call | solution.py:566
  25.8 107.6 %all_to_all.10.slots = bf16[32,1072,128]{2,1,0:T(8,128)(2,1)} all-to-all(bf16[32,1072,128]{2,1,0:T(8,128)(2,1)} %fill_slots.1), channel_id=1, replica_groups=mesh['branch'=32,'tensor'=4] {'branch'}, dimensions={0} | all-to-all | bytes 17563648 | tf_op jit(solution)/shard_map/all_to_all | solution.py:694
  133.4 6.5 %second_half.1 = (f32[64,512]{1,0:T(8,128)S(1)}, f32[64,512]{1,0:T(8,128)S(1)}, f32[64,512]{1,0:T(8,128)S(1)}, f32[64,512]{1,0:T(8,128)S(1)}, f32[16,40,128]{2,1...) custom-call(s32[16]{0:T(128)S(1)} %get-tuple-element.50.slot_ref, ...), custom_call_target="tpu_custom_call" | custom-call | tf_op jit(solution)/shard_map/second_half/pallas_call | solution.py:585
  139.9 1.7 %collective-permute-start = (f32[64,512]{1,0:T(8,128)S(1)}, f32[64,512]{1,0:T(8,128)S(1)}, u32[]{:S(2)}, u32[]{:S(2)}) collective-permute-start(f32[64,512]{1,0:T(8,128)S(1)} %get-tuple-element.38), channel_id=1, source_target_pairs={{0,1},{1,2},{2,3},{3,0},{4,5},{5,6},{6,7},{7,4},{8,9},{9,10},{10,1... | collective-permute-start | bytes 393224 | tf_op jit(solution)/shard_map/ppermute | solution.py:638
  141.6 2.8 %collective-permute-start.1 = (f32[64,512]{1,0:T(8,128)S(1)}, f32[64,512]{1,0:T(8,128)S(1)}, u32[]{:S(2)}, u32[]{:S(2)}) collective-permute-start(f32[64,512]{1,0:T(8,128)S(1)} %get-tuple-element.39), channel_id=1, source_target_pairs={{0,2},{1,3},{2,0},{3,1},{4,6},{5,7},{6,4},{7,5},{8,10},{9,11},{10,... | collective-permute-start | bytes 393224 | tf_op jit(solution)/shard_map/ppermute | solution.py:638
  144.4 1.4 collective-permute-start.2
  145.8 3.8 %last_memory.1 = (bf16[16,1024,128]{2,1,0:T(8,128)(2,1)}, bf16[3,16,512]{2,1,0:T(8,128)(2,1)}, bf16[3,16,512]{2,1,0:T(8,128)(2,1)}, bf16[3,16,1024]{2,1,0:T(8,128)(2,1)}) custom-call(f32[16,40,128]{2,1,0:T(8,128)S(1)} %get-tuple-element.41.update_ref, bf16[16,16,128]{2,1,0:T(8,128)(2,1)S(1)} %get-tuple-element.42.last_ref, ...), custom_call_target="tpu_custom_call" | custom-call | tf_op jit(solution)/shard_map/last_memory/pallas_call | solution.py:614
  149.6 0.0 collective-permute-done
  149.6 1.3 collective-permute-done.1
  150.8 0.0 collective-permute-done.2
  150.8 0.7 add_convert_fusion
  (1 shorter events, 0.0 us)
Async XLA Ops:
  2.1 16.8 %all-to-all-start = ((s32[32,1,1]{2,1,0:T(1,128)}), s32[32,1,1]{2,1,0:T(1,128)S(1)}, u32[]{:S(2)}, u32[]{:S(2)}) async-start(s32[32,1,1]{2,1,0:T(1,128)} %copy.25), calls=%async_computation | async-start | bytes 32768 | tf_op jit(solution)/shard_map/all_to_all | solution.py:667
  139.9 9.7 %collective-permute-start = (f32[64,512]{1,0:T(8,128)S(1)}, f32[64,512]{1,0:T(8,128)S(1)}, u32[]{:S(2)}, u32[]{:S(2)}) collective-permute-start(f32[64,512]{1,0:T(8,128)S(1)} %get-tuple-element.38), channel_id=1, source_target_pairs={{0,1},{1,2},{2,3},{3,0},{4,5},{5,6},{6,7},{7,4},{8,9},{9,10},{10,1... | collective-permute-start | bytes 393224 | tf_op jit(solution)/shard_map/ppermute | solution.py:638
  141.6 9.2 %collective-permute-start.1 = (f32[64,512]{1,0:T(8,128)S(1)}, f32[64,512]{1,0:T(8,128)S(1)}, u32[]{:S(2)}, u32[]{:S(2)}) collective-permute-start(f32[64,512]{1,0:T(8,128)S(1)} %get-tuple-element.39), channel_id=1, source_target_pairs={{0,2},{1,3},{2,0},{3,1},{4,6},{5,7},{6,4},{7,5},{8,10},{9,11},{10,... | collective-permute-start | bytes 393224 | tf_op jit(solution)/shard_map/ppermute | solution.py:638
  144.4 6.4 %collective-permute-start.2 = (f32[64,512]{1,0:T(8,128)S(1)}, f32[64,512]{1,0:T(8,128)S(1)}, u32[]{:S(2)}, u32[]{:S(2)}) collective-permute-start(f32[64,512]{1,0:T(8,128)S(1)} %get-tuple-element.40), channel_id=1, source_target_pairs={{0,3},{1,0},{2,1},{3,2},{4,7},{5,4},{6,5},{7,6},{8,11},{9,8},{10,9... | collective-permute-start | bytes 393224 | tf_op jit(solution)/shard_map/ppermute | solution.py:638

commit v2 on v1

--- a/solution.py
+++ b/solution.py
@@ -18,7 +18,7 @@
 VMEM_BYTES = 48 * 1024 * 1024
 CHUNK = 4
 PARTS = 4
-GROUP = 4
+GROUP = 8
 f32 = jnp.float32
 bf16 = jnp.bfloat16
 
@@ -42,6 +42,10 @@
     tap, place = row // WIDE, row % WIDE
     origin = tap * SLIM + jnp.where(place < 2 * HEADS, place // 2, place - HEADS)
     return jnp.where(origin == column, 1.0, 0.0).astype(bf16)
+
+
+def spread(target, start, h, block):
+    target[pl.ds(start * HEADS + h, block.shape[0], stride=HEADS), :] = block
 
 
 def part_of(ref, index, first, count):
@@ -117,7 +121,9 @@
         read1 = decay1 * kept + inner(query1, key1) * change1
         for step, read in enumerate((read0, read1)):
             scale = lax.rsqrt(jnp.mean(read * read, axis=-1, keepdims=True) + 1e-06)
-            normed = read * scale * shaped(gate(step, first))
+            normed = read * scale
+            if gate is not None:
+                normed = normed * shaped(gate(step, first))
             start = (step * ROWS + first) * HEADS
             normed_buf[start : start + CHUNK * HEADS, :] = normed.reshape(CHUNK * HEADS, DV)
         for i, value in enumerate((key0, key1, decay1 * change0, change1, decay0 * decay1)):
@@ -161,15 +167,15 @@
 
 
 def first_kernel(
-    x, gain, tail_query, tail_key, tail_value, conv_query, conv_key, conv_value,
-    w_query, w_key, w_value, w_gate, w_beta, w_decay, decay_log, dt_bias, state,
-    late_query_ref, late_key_ref, late_value_ref, late_gate_ref, late_strength_ref, late_forget_ref,
-    raw_ref, stored_ref, conv_ref, normed_ref, update_ref,
-    x_buf, gain_buf, tail_query_buf, tail_key_buf, tail_value_buf,
+    x, tail_query, tail_key, tail_value, conv_query, conv_key, conv_value,
+    w_query, w_key, w_value, w_beta, w_decay, decay_log, dt_bias, state,
+    late_query_ref, late_key_ref, late_value_ref, late_strength_ref, late_forget_ref,
+    raw_ref, stored_ref, conv_ref, normed_buf, update_ref,
+    x_buf, tail_query_buf, tail_key_buf, tail_value_buf,
     conv_query_buf, conv_key_buf, conv_value_buf,
-    query_buf, key_buf, value_weight_buf, gate_weight_buf, beta_buf, decay_buf, decay_ref, bias_ref, state_buf,
-    window_query, window_key, window_value, gate_all, strength_all, forget_all, stored_buf,
-    vector_buf, value_buf, found_buf, normed_buf,
+    query_buf, key_buf, value_weight_buf, beta_buf, decay_buf, decay_ref, bias_ref, state_buf,
+    window_query, window_key, window_value, strength_all, forget_all, stored_buf,
+    vector_buf, value_buf, found_buf,
     small_sem, weight_sem, state_sem,
 ):
     rows = x_buf.shape[0]
@@ -180,7 +186,6 @@
                 (x, x_buf),
                 (w_beta, beta_buf),
                 (w_decay, decay_buf),
-                (gain, gain_buf),
                 (tail_query, tail_query_buf),
                 (tail_key, tail_key_buf),
                 (tail_value, tail_value_buf),
@@ -200,13 +205,12 @@
             (w_query, query_buf, DK),
             (w_key, key_buf, DK),
             (w_value, value_weight_buf, 2 * DV),
-            (w_gate, gate_weight_buf, 2 * DV),
         )
         copies = []
         for i, (hbm, buf, width) in enumerate(pieces):
             part = pl.ds(j * width, width)
             copies.append(
-                pltpu.make_async_copy(hbm.at[:, part], buf.at[:, part], weight_sem.at[4 * j + i])
+                pltpu.make_async_copy(hbm.at[:, part], buf.at[:, part], weight_sem.at[3 * j + i])
             )
         return copies
 
@@ -233,9 +237,6 @@
         bias = jnp.where(head == h, bias_ref[h], bias)
     rate = -jnp.exp(rate)
     x_all = x_buf[...]
-
-    def spread(target, start, h, block):
-        target[pl.ds(start * HEADS + h, block.shape[0], stride=HEADS), :] = block
 
     across = (((1,), (1,)), ((), ()))
     beta = lax.dot_general(x_all, beta_buf[...], across, preferred_element_type=f32)
@@ -279,7 +280,6 @@
         query = dot(x_all, query_buf[:, one]).astype(bf16)
         key = dot(x_all, key_buf[:, one]).astype(bf16)
         value = dot(x_all, value_weight_buf[:, two]).astype(bf16)
-        gate = dot(x_all, gate_weight_buf[:, two])
         raw_ref[:, j * DK : (j + 1) * DK] = query[2 * ROWS :]
         raw_ref[:, (KEYS + j) * DK : (KEYS + j + 1) * DK] = key[2 * ROWS :]
         raw_ref[:, 2 * (KEYS + j) * DK : 2 * (KEYS + j + 1) * DK] = value[2 * ROWS :]
@@ -287,7 +287,6 @@
         old_query = tail_query_buf[:, :, one].reshape(history, DK).astype(f32)
         old_key = tail_key_buf[:, :, one].reshape(history, DK).astype(f32)
         old_value = tail_value_buf[:, :, two].reshape(history, 2 * DV).astype(f32)
-        gate = gate * jax.nn.sigmoid(gate)
         keep(j, old_query, query)
         keep(KEYS + j, old_key, key)
         for i in range(2):
@@ -296,13 +295,11 @@
             place(window_key, h, old_key, key)
             place(window_value, h, old_value[:, half], value[:, half])
             keep(2 * KEYS + h, old_value[:, half], value[:, half])
-            spread(gate_all, 0, h, gate[:, half] * gain_buf[...])
 
     late = (history + 2 * ROWS) * HEADS
     late_query_ref[...] = window_query[late:, :]
     late_key_ref[...] = window_key[late:, :]
     late_value_ref[...] = window_value[late:, :]
-    late_gate_ref[...] = gate_all[2 * ROWS * HEADS :, :]
     late_strength_ref[...] = strength_all[2 * ROWS * HEADS :, :]
     late_forget_ref[...] = forget_all[2 * ROWS * HEADS :, :]
     stored_ref[...] = stored_buf[...].reshape(stored_ref.shape).astype(bf16)
@@ -323,14 +320,52 @@
     finish(
         lambda step, first: part_of(strength_all, step, first, CHUNK),
         lambda step, first: part_of(forget_all, step, first, CHUNK),
-        lambda step, first: part_of(gate_all, step, first, CHUNK),
+        None,
         vector_buf,
         value_buf,
         found_buf,
         normed_buf,
         update_ref,
     )
-    flatten_heads(normed_buf, normed_ref)
+
+
+def gate_kernel(
+    x, gain, w_gate, read_ref, late_ref, normed_ref, x_buf, gain_buf, weight_buf, gate_all, small_sem, weight_sem
+):
+    small = [
+        pltpu.make_async_copy(x, x_buf, small_sem.at[0]),
+        pltpu.make_async_copy(gain, gain_buf, small_sem.at[1]),
+    ]
+    for copy in small:
+        copy.start()
+    copies = []
+    for j in range(KEYS):
+        part = pl.ds(2 * j * DV, 2 * DV)
+        copies.append(
+            pltpu.make_async_copy(w_gate.at[:, part], weight_buf.at[:, part], weight_sem.at[j])
+        )
+        copies[j].start()
+    for copy in small:
+        copy.wait()
+    for j in range(KEYS):
+        copies[j].wait()
+        gate = dot(x_buf[...], weight_buf[:, 2 * j * DV : 2 * (j + 1) * DV])
+        gate = gate * jax.nn.sigmoid(gate)
+        for i in range(2):
+            spread(gate_all, 0, 2 * j + i, gate[:, i * DV : (i + 1) * DV] * gain_buf[...])
+    half = 2 * ROWS * HEADS
+    late_ref[...] = gate_all[half:, :]
+    gate_all[:half, :] = gate_all[:half, :] * read_ref[...]
+    flatten_heads(gate_all, normed_ref)
+
+
+def ask_kernel(parent_ref, wanted_ref):
+    slot = lax.broadcasted_iota(jnp.int32, wanted_ref.shape, 0)
+    wanted = jnp.full(wanted_ref.shape, -1, jnp.int32)
+    for row in range(ROWS):
+        parent = parent_ref[row]
+        wanted = jnp.where(slot == parent // ROWS, parent % ROWS, wanted)
+    wanted_ref[...] = wanted
 
 
 def send_kernel(
@@ -385,7 +420,7 @@
 
 
 def second_kernel(
-    slot_ref, late_query, late_key, late_value, late_gate, late_strength, late_forget, conv_ref, early_ref, slots, w_out,
+    parent_ref, late_query, late_key, late_value, late_strength, late_forget, late_gate, conv_ref, early_ref, slots, w_out,
     *refs,
 ):
     sums = refs[:PARTS]
@@ -397,12 +432,12 @@
     ) = refs[PARTS:]
     def load_tail(row):
         return pltpu.make_async_copy(
-            slots.at[slot_ref[row], pl.ds(BODY, SLOT - BODY)], tail_buf.at[row], tail_sem.at[row]
+            slots.at[parent_ref[row] // ROWS, pl.ds(BODY, SLOT - BODY)], tail_buf.at[row], tail_sem.at[row]
         )
 
     def load(row):
         return pltpu.make_async_copy(
-            slots.at[slot_ref[row], pl.ds(0, BODY)], memory_buf.at[row], memory_sem.at[row]
+            slots.at[parent_ref[row] // ROWS, pl.ds(0, BODY)], memory_buf.at[row], memory_sem.at[row]
         )
 
     for row in range(ROWS):
@@ -426,11 +461,11 @@
     for row in range(ROWS):
         tails = tail_buf[row]
         last_ref[row] = tails[2 * SLIM :]
-        spread = dot(wide, tails)
+        spaced = dot(wide, tails)
         for tap in range(TAPS - 1):
             for kind, window in enumerate((window_query, window_key, window_value)):
                 start = tap * WIDE + kind * HEADS
-                window[(tap * ROWS + row) * HEADS : (tap * ROWS + row + 1) * HEADS, :] = spread[
+                window[(tap * ROWS + row) * HEADS : (tap * ROWS + row + 1) * HEADS, :] = spaced[
                     start : start + HEADS
                 ]
     windows = (window_query, window_key, window_value)
@@ -464,7 +499,7 @@
         load_out(shift).wait()
     normed = normed_ref[...]
     for shift in range(PARTS):
-        sums[shift][...] = dot(normed, out_buf[shift])
+        sums[shift][...] = dot(normed, out_buf[shift]).astype(sums[shift].dtype)
 
 
 def final_kernel(
@@ -524,21 +559,32 @@
     ]
 
 
+def ask(parents, groups):
+    return pl.pallas_call(
+        ask_kernel,
+        in_specs=[SMEM],
+        out_specs=VMEM,
+        out_shape=shape((groups, 1, DV), jnp.int32),
+        name="ask",
+    )(parents)
+
+
 def first_half(arrays, state):
     rows = arrays[0].shape[0]
     late = rows // 2
     window = pltpu.VMEM(((TAPS - 1) * ROWS * HEADS + rows * HEADS, DV), f32)
     wide = pltpu.VMEM((rows * HEADS, DV), f32)
+    vectors, values, found, _ = work_buffers()
     return pl.pallas_call(
         first_kernel,
         in_specs=[HBM] * (len(arrays) + 1),
-        out_specs=[VMEM] * 11,
+        out_specs=[VMEM] * 10,
         out_shape=(
-            *[shape((late * HEADS, DV), f32)] * 6,
+            *[shape((late * HEADS, DV), f32)] * 5,
             shape((late, SLIM * DV), bf16),
             shape((ROWS, (TAPS - 1) * SLIM, DV), bf16),
             shape((3, TAPS, HEADS, DV), f32),
-            shape((late, HEADS * DV), bf16),
+            shape((late * HEADS, DV), f32),
             shape((ROWS, 5 * HEADS, DV), f32),
         ),
         scratch_shapes=[
@@ -550,16 +596,40 @@
             window,
             wide,
             wide,
-            wide,
             pltpu.VMEM((ROWS * (TAPS - 1) * SLIM, DV), f32),
-            *work_buffers(),
-            pltpu.SemaphoreType.DMA((12,)),
-            pltpu.SemaphoreType.DMA((4 * KEYS,)),
+            vectors,
+            values,
+            found,
+            pltpu.SemaphoreType.DMA((len(arrays) - 3,)),
+            pltpu.SemaphoreType.DMA((3 * KEYS,)),
             pltpu.SemaphoreType.DMA((ROWS,)),
         ],
         compiler_params=PARAMS,
         name="first_half",
     )(*[in_hbm(array) for array in arrays], in_hbm(state))
+
+
+def apply_gates(x, norm_gain, w_gate, read):
+    rows = x.shape[0]
+    return pl.pallas_call(
+        gate_kernel,
+        in_specs=[HBM] * 3 + [VMEM],
+        out_specs=[VMEM] * 2,
+        out_shape=(
+            shape((rows * HEADS // 2, DV), f32),
+            shape((rows // 2, HEADS * DV), bf16),
+        ),
+        scratch_shapes=[
+            buffer(x),
+            buffer(norm_gain),
+            buffer(w_gate),
+            pltpu.VMEM((rows * HEADS, DV), f32),
+            pltpu.SemaphoreType.DMA((2,)),
+            pltpu.SemaphoreType.DMA((KEYS,)),
+        ],
+        compiler_params=PARAMS,
+        name="apply_gates",
+    )(in_hbm(x), in_hbm(norm_gain), in_hbm(w_gate), read)
 
 
 def fill_slots(wanted, update, tails, state):
@@ -579,7 +649,7 @@
     )(wanted, update, tails, in_hbm(state))
 
 
-def second_half(slot_of_row, late, conv, normed, slots, w_out):
+def second_half(parents, late, conv, normed, slots, w_out):
     window = pltpu.VMEM(((TAPS - 1) * ROWS * HEADS, DV), f32)
     rows, width = 2 * normed.shape[0], w_out.shape[1] // PARTS
     *sums, update, last, memory = pl.pallas_call(
@@ -587,7 +657,8 @@
         in_specs=[SMEM] + [VMEM] * 8 + [HBM] * 2,
         out_specs=[VMEM] * (PARTS + 3),
         out_shape=(
-            *[shape((rows, width), f32)] * PARTS,
+            shape((rows, width), f32),
+            *[shape((rows, width), bf16)] * (PARTS - 1),
             shape((ROWS, 5 * HEADS, DV), f32),
             shape((ROWS, SLIM, DV), bf16),
             shape((ROWS, BODY, DV), bf16),
@@ -606,7 +677,7 @@
         ],
         compiler_params=PARAMS,
         name="second_half",
-    )(slot_of_row, *late, conv, normed, in_hbm(slots), in_hbm(w_out))
+    )(parents, *late, conv, normed, in_hbm(slots), in_hbm(w_out))
     return sums, update, last, memory
 
 
@@ -635,7 +706,7 @@
     total = blocks[0]
     for shift in range(1, PARTS):
         pairs = [(i, (i + shift) % PARTS) for i in range(PARTS)]
-        total = total + lax.ppermute(blocks[shift], "tensor", pairs)
+        total = total + lax.ppermute(blocks[shift], "tensor", pairs).astype(f32)
     return total.astype(bf16)
 
 
@@ -660,19 +731,14 @@
     tail_value,
     parents,
 ):
-    groups = lax.axis_size("branch")
-    source, offset = parents // ROWS, parents % ROWS
-    hits = source[:, None] == jnp.arange(groups, dtype=jnp.int32)[None, :]
-    wanted = jnp.sum(jnp.where(hits, offset[:, None] + 1, 0), axis=0) - 1
-    requested = lax.all_to_all(
-        wanted.reshape(groups, 1, 1), "branch", split_axis=0, concat_axis=0, tiled=True
-    )
-
+    wanted = ask(parents, lax.axis_size("branch"))
+    requested = lax.all_to_all(wanted, "branch", split_axis=0, concat_axis=0, tiled=True)
+
+    x = inputs.reshape(-1, inputs.shape[-1])
     flat_state = state.reshape(ROWS, BODY, DV)
-    *late, raw, stored_tails, conv, normed, update = first_half(
+    *late, raw, stored_tails, conv, read, update = first_half(
         (
-            inputs.reshape(-1, inputs.shape[-1]),
-            norm_gain[None],
+            x,
             tail_query.transpose(1, 0, 2),
             tail_key.transpose(1, 0, 2),
             tail_value.transpose(1, 0, 2),
@@ -682,7 +748,6 @@
             w_query,
             w_key,
             w_value,
-            w_gate_z,
             w_beta.T,
             w_decay.T,
             decay_log,
@@ -692,8 +757,10 @@
     )
     shipped = fill_slots(requested, update, stored_tails, flat_state)
     arrived = lax.all_to_all(shipped, "branch", split_axis=0, concat_axis=0, tiled=True)
-
-    sums, update, last, memory = second_half(source, late, conv, normed, arrived, w_out)
+    late_gate, normed = apply_gates(x, norm_gain[None], w_gate_z, read)
+    sums, update, last, memory = second_half(
+        parents, (*late, late_gate), conv, normed, arrived, w_out
+    )
     out_rows = sum_heads(sums).reshape(inputs.shape[0], ROWS, -1)
     final_state, *final_tails = last_memory(update, last, raw, memory)
     return (

time: 152 us -> 160 us (1.053)
  blocking collectives: 108 us -> 0 us
  waiting for transfers between devices: 1.26 us -> 107 us
  starting transfers between devices: 14.1 us -> 21.7 us
  Pallas kernels: 25.7 us -> 29.1 us
    all_to_all x1 -> x0, blocking collectives: 108 us -> none  [per_device(): lax.all_to_all(shipped, 'branch', split_axis=0, concat_axis=0, tiled=True)]
    all_to_all x1 -> x2, waiting for transfers between devices: 0.01 us -> 107 us  [the longest x1 107 us: per_device(): lax.all_to_all(shipped, 'branch', split_axis=0, concat_axis=0, tiled=True)]
    all_to_all x1 -> x2, starting transfers between devices: 8.24 us -> 15.8 us  [the longest x1 8.24 us: per_device(): lax.all_to_all(wanted, 'branch', split_axis=0, concat_axis=0, tiled=True)]
    pallas_call x0 -> x2, Pallas kernels: none -> 5 us  [the longest x1 3.57 us: apply_gates(): pl.pallas_call(gate_kernel, in_specs=[HBM] * 3 + [VMEM], out_specs=[VMEM]...]
  transfers between devices with their start and end apart: 4 -> 5, of which waited for: 1 -> 1; matrix products, arithmetic and copies ran while one was open for 0% -> 0% of each run, Pallas kernels for 8% -> 9%
where the time goes in v2:
time: 160 us
  waiting for transfers between devices  107 us (67%)
  Pallas kernels  29.1 us (18%)
  starting transfers between devices  21.7 us (14%)
    all_to_all x1, waiting for transfers between devices, per_device(): lax.all_to_all(shipped, 'branch', split_axis=0, concat_axis=0, tiled=True)  107 us
    all_to_all x1, starting transfers between devices, per_device(): lax.all_to_all(wanted, 'branch', split_axis=0, concat_axis=0, tiled=True)  8.24 us
    pallas_call x1, Pallas kernels, first_half(): pl.pallas_call(first_kernel, in_specs=[HBM] * (len(arrays) + 1), out_spec...  7.79 us
    all_to_all x1, starting transfers between devices, per_device(): lax.all_to_all(shipped, 'branch', split_axis=0, concat_axis=0, tiled=True)  7.57 us
    pallas_call x1, Pallas kernels, fill_slots(): pl.pallas_call(send_kernel, in_specs=[SMEM, VMEM, VMEM, HBM], out_specs=H...  6.41 us
    pallas_call x1, Pallas kernels, second_half(): pl.pallas_call(second_kernel, in_specs=[SMEM] + [VMEM] * 8 + [HBM] * 2, o...  6.22 us
    ppermute x3, starting transfers between devices, sum_heads(): total = total + lax.ppermute(blocks[shift], 'tensor', pairs).astype(f32)  5.89 us
    pallas_call x1, Pallas kernels, last_memory(): pl.pallas_call(final_kernel, in_specs=[VMEM] * 4, out_specs=[HBM] + [VMEM...  3.69 us
  transfers between devices with their start and end apart: 5, of which 1 were waited for; matrix products, arithmetic and copies ran while one was open for 0% of the time, Pallas kernels for 9%

profile of v2, /device:TPU:0, one launch (start us, length us, event | category | flops | bytes accessed | tf_op | source)
XLA Modules:
  0.0 159.6 jit_solution(6300514952307248104)
XLA Ops:
  0.6 1.4 ask.1
  2.1 8.2 %all-to-all-start = ((s32[32,1,128]{2,1,0:T(1,128)}), s32[32,1,128]{2,1,0:T(1,128)S(1)}, u32[]{:S(2)}, u32[]{:S(2)}) async-start(s32[32,1,128]{2,1,0:T(1,128)} %ask.1), calls=%async_computation | async-start | bytes 32768 | tf_op jit(solution)/shard_map/all_to_all | solution.py:735
  10.3 7.8 %first_half.1 = (f32[256,128]{1,0:T(8,128)S(1)}, f32[256,128]{1,0:T(8,128)S(1)}, f32[256,128]{1,0:T(8,128)S(1)}, f32[256,128]{1,0:T(8,128)S(1)}, f32[256,128]{1,...) custom-call(bf16[64,2048]{1,0:T(8,128)(2,1)} %bitcast.15, ...), custom_call_target="tpu_custom_call" | custom-call | tf_op jit(solution)/shard_map/first_half/pallas_call | solution.py:578
  18.1 0.0 all-to-all-done.wanted_ref
  18.1 6.4 %fill_slots.1 = bf16[32,1072,128]{2,1,0:T(8,128)(2,1)} custom-call(s32[32,1,128]{2,1,0:T(1,128)S(1)} %all-to-all-done.wanted_ref, f32[16,40,128]{2,1,0:T(8,128)S(1)} %get-tuple-element.37.update_ref, bf16[16,48,128]{2,1,0:T(8,128)(2,1)S(1)} %get-tuple-element.38.tails_ref, bf16[16,1024,128]{2,1,0:T(8,128)(2,1)} %bitcast.14), custom_call_target="tpu_custom_call" | custom-call | tf_op jit(solution)/shard_map/fill_slots/pallas_call | solution.py:636
  24.5 7.6 %all-to-all-start.1 = ((bf16[32,1072,128]{2,1,0:T(8,128)(2,1)}), bf16[32,1072,128]{2,1,0:T(8,128)(2,1)}, u32[]{:S(2)}, u32[]{:S(2)}) async-start(bf16[32,1072,128]{2,1,0:T(8,128)(2,1)} %fill_slots.1), calls=%async_computation.1 | async-start | bytes 17563648 | tf_op jit(solution)/shard_map/all_to_all | solution.py:759
  32.1 0.0 copy-start
  32.1 3.6 %apply_gates.1 = (f32[256,128]{1,0:T(8,128)S(1)}, bf16[32,1024]{1,0:T(8,128)(2,1)S(1)}) custom-call(bf16[64,2048]{1,0:T(8,128)(2,1)} %bitcast.16, f32[1,128]{1,0:T(1,128)} %bitcast.23, bf16[2048,1024]{1,0:T(8,128)(2,1)} %w_gate.1, f32[256,128]{1,0:T(8,128)S(1)} %get-tuple-element.33.read_ref), custom_call_target="tpu_custom_call" | custom-call | tf_op jit(solution)/shard_map/apply_gates/pallas_call | solution.py:614
  35.7 107.4 %all-to-all-done.1.slots = bf16[32,1072,128]{2,1,0:T(8,128)(2,1)} async-done(((bf16[32,1072,128]{2,1,0:T(8,128)(2,1)}), bf16[32,1072,128]{2,1,0:T(8,128)(2,1)}, u32[]{:S(2)}, u32[]{:S(2)}) %all-to-all-start.1) | async-done | bytes 8781856 | tf_op jit(solution)/shard_map/all_to_all | solution.py:759
  143.1 0.0 copy-done
  143.1 6.2 %second_half.1 = (f32[64,512]{1,0:T(8,128)S(1)}, bf16[64,512]{1,0:T(8,128)(2,1)S(1)}, bf16[64,512]{1,0:T(8,128)(2,1)S(1)}, bf16[64,512]{1,0:T(8,128)(2,1)S(1)}, ...) custom-call(s32[16]{0:T(128)S(1)} %copy-done, ...), custom_call_target="tpu_custom_call" | custom-call | tf_op jit(solution)/shard_map/second_half/pallas_call | solution.py:655
  149.3 1.8 %collective-permute-start = (bf16[64,512]{1,0:T(8,128)(2,1)S(1)}, bf16[64,512]{1,0:T(8,128)(2,1)S(1)}, u32[]{:S(2)}, u32[]{:S(2)}) collective-permute-start(bf16[64,512]{1,0:T(8,128)(2,1)S(1)} %get-tuple-element.40), channel_id=1, source_target_pairs={{0,1},{1,2},{2,3},{3,0},{4,5},{5,6},{6,7},{7,4},{8,9},{9,10},{10,1... | collective-permute-start | bytes 196616 | tf_op jit(solution)/shard_map/ppermute | solution.py:709
  151.1 3.0 %collective-permute-start.1 = (bf16[64,512]{1,0:T(8,128)(2,1)S(1)}, bf16[64,512]{1,0:T(8,128)(2,1)S(1)}, u32[]{:S(2)}, u32[]{:S(2)}) collective-permute-start(bf16[64,512]{1,0:T(8,128)(2,1)S(1)} %get-tuple-element.41), channel_id=1, source_target_pairs={{0,2},{1,3},{2,0},{3,1},{4,6},{5,7},{6,4},{7,5},{8,10},{9,11},{10,... | collective-permute-start | bytes 196616 | tf_op jit(solution)/shard_map/ppermute | solution.py:709
  154.1 1.1 collective-permute-start.2
  155.2 3.7 %last_memory.1 = (bf16[16,1024,128]{2,1,0:T(8,128)(2,1)}, bf16[3,16,512]{2,1,0:T(8,128)(2,1)}, bf16[3,16,512]{2,1,0:T(8,128)(2,1)}, bf16[3,16,1024]{2,1,0:T(8,128)(2,1)}) custom-call(f32[16,40,128]{2,1,0:T(8,128)S(1)} %get-tuple-element.43.update_ref, bf16[16,16,128]{2,1,0:T(8,128)(2,1)S(1)} %get-tuple-element.44.last_ref, ...), custom_call_target="tpu_custom_call" | custom-call | tf_op jit(solution)/shard_map/last_memory/pallas_call | solution.py:685
  158.9 0.0 collective-permute-done
  158.9 0.0 collective-permute-done.1
  158.9 0.0 collective-permute-done.2
  158.9 0.7 add_convert_fusion
Async XLA Ops:
  2.1 16.1 %all-to-all-start = ((s32[32,1,128]{2,1,0:T(1,128)}), s32[32,1,128]{2,1,0:T(1,128)S(1)}, u32[]{:S(2)}, u32[]{:S(2)}) async-start(s32[32,1,128]{2,1,0:T(1,128)} %ask.1), calls=%async_computation | async-start | bytes 32768 | tf_op jit(solution)/shard_map/all_to_all | solution.py:735
  24.5 118.5 %all-to-all-start.1 = ((bf16[32,1072,128]{2,1,0:T(8,128)(2,1)}), bf16[32,1072,128]{2,1,0:T(8,128)(2,1)}, u32[]{:S(2)}, u32[]{:S(2)}) async-start(bf16[32,1072,128]{2,1,0:T(8,128)(2,1)} %fill_slots.1), calls=%async_computation.1 | async-start | bytes 17563648 | tf_op jit(solution)/shard_map/all_to_all | solution.py:759
  32.1 111.0 %copy-start = (s32[16]{0:T(128)S(1)}, s32[16]{0:T(128)}, u32[]{:S(2)}) copy-start(s32[16]{0:T(128)} %parent_ref.3) | copy-start | bytes 196
  149.3 9.6 %collective-permute-start = (bf16[64,512]{1,0:T(8,128)(2,1)S(1)}, bf16[64,512]{1,0:T(8,128)(2,1)S(1)}, u32[]{:S(2)}, u32[]{:S(2)}) collective-permute-start(bf16[64,512]{1,0:T(8,128)(2,1)S(1)} %get-tuple-element.40), channel_id=1, source_target_pairs={{0,1},{1,2},{2,3},{3,0},{4,5},{5,6},{6,7},{7,4},{8,9},{9,10},{10,1... | collective-permute-start | bytes 196616 | tf_op jit(solution)/shard_map/ppermute | solution.py:709
  151.1 7.8 %collective-permute-start.1 = (bf16[64,512]{1,0:T(8,128)(2,1)S(1)}, bf16[64,512]{1,0:T(8,128)(2,1)S(1)}, u32[]{:S(2)}, u32[]{:S(2)}) collective-permute-start(bf16[64,512]{1,0:T(8,128)(2,1)S(1)} %get-tuple-element.41), channel_id=1, source_target_pairs={{0,2},{1,3},{2,0},{3,1},{4,6},{5,7},{6,4},{7,5},{8,10},{9,11},{10,... | collective-permute-start | bytes 196616 | tf_op jit(solution)/shard_map/ppermute | solution.py:709
  154.1 4.9 %collective-permute-start.2 = (bf16[64,512]{1,0:T(8,128)(2,1)S(1)}, bf16[64,512]{1,0:T(8,128)(2,1)S(1)}, u32[]{:S(2)}, u32[]{:S(2)}) collective-permute-start(bf16[64,512]{1,0:T(8,128)(2,1)S(1)} %get-tuple-element.42), channel_id=1, source_target_pairs={{0,3},{1,0},{2,1},{3,2},{4,7},{5,4},{6,5},{7,6},{8,11},{9,8},{10,9... | collective-permute-start | bytes 196616 | tf_op jit(solution)/shard_map/ppermute | solution.py:709

commit v3 on v1

--- a/solution.py
+++ b/solution.py
@@ -18,7 +18,9 @@
 VMEM_BYTES = 48 * 1024 * 1024
 CHUNK = 4
 PARTS = 4
-GROUP = 4
+GROUP = 8
+AHEAD = 2
+SHIP = 8
 f32 = jnp.float32
 bf16 = jnp.bfloat16
 
@@ -42,6 +44,10 @@
     tap, place = row // WIDE, row % WIDE
     origin = tap * SLIM + jnp.where(place < 2 * HEADS, place // 2, place - HEADS)
     return jnp.where(origin == column, 1.0, 0.0).astype(bf16)
+
+
+def spread(target, start, h, block):
+    target[pl.ds(start * HEADS + h, block.shape[0], stride=HEADS), :] = block
 
 
 def part_of(ref, index, first, count):
@@ -68,10 +74,9 @@
                 vector_buf[there, place * HEADS : (place + 1) * HEADS, :] = unit
 
 
-def recall(wait, memory, vector_buf, found_buf):
+def recall(rows, memory, vector_buf, found_buf):
     head = lax.broadcasted_iota(jnp.int32, (HEADS, DV), 0)
-
-    def one(row):
+    for row in rows:
         high, low = split(vector_buf[row])
         left = jnp.concatenate([high, low], axis=0).astype(bf16)
         found = [jnp.zeros((HEADS, DV), f32)] * 4
@@ -85,43 +90,34 @@
                 found[i] = jnp.where(head == h + 1, block[:, DV:], found[i])
         found_buf[row] = jnp.concatenate(found, axis=0)
 
-    def group(index, carry):
-        for i in range(GROUP):
-            wait(index * GROUP + i)
-        for i in range(GROUP):
-            one(index * GROUP + i)
-        return carry
-
-    lax.fori_loop(0, ROWS // GROUP, group, 0)
-
-
-def finish(strength, decay, gate, vector_buf, value_buf, found_buf, normed_buf, update_ref):
-    for first in range(0, ROWS, CHUNK):
-        there = slice(first, first + CHUNK)
-
-        def piece(ref, i):
-            return ref[there, i * HEADS : (i + 1) * HEADS, :]
-
-        def shaped(value):
-            return value.reshape(CHUNK, HEADS, DV)
-
-        key0, query0, key1, query1 = [piece(vector_buf, i) for i in range(4)]
-        found0, found1, found2, found3 = [piece(found_buf, i) for i in range(4)]
-        strength0, strength1 = [shaped(strength(step, first)) for step in range(2)]
-        decay0, decay1 = [shaped(decay(step, first)) for step in range(2)]
-        change0 = (value_buf[0, there] - decay0 * found0) * strength0
-        read0 = decay0 * found1 + inner(query0, key0) * change0
-        kept = decay0 * found2 + inner(key1, key0) * change0
-        change1 = (value_buf[1, there] - decay1 * kept) * strength1
-        kept = decay0 * found3 + inner(query1, key0) * change0
-        read1 = decay1 * kept + inner(query1, key1) * change1
-        for step, read in enumerate((read0, read1)):
-            scale = lax.rsqrt(jnp.mean(read * read, axis=-1, keepdims=True) + 1e-06)
-            normed = read * scale * shaped(gate(step, first))
-            start = (step * ROWS + first) * HEADS
-            normed_buf[start : start + CHUNK * HEADS, :] = normed.reshape(CHUNK * HEADS, DV)
-        for i, value in enumerate((key0, key1, decay1 * change0, change1, decay0 * decay1)):
-            update_ref[there, i * HEADS : (i + 1) * HEADS, :] = value
+
+def finish(first, strengths, decays, gates, vector_buf, value_buf, found_buf, normed_buf, update_buf):
+    there = slice(first, first + CHUNK)
+
+    def piece(ref, i):
+        return ref[there, i * HEADS : (i + 1) * HEADS, :]
+
+    def steps(ref):
+        return [part_of(ref, step, first, CHUNK).reshape(CHUNK, HEADS, DV) for step in range(2)]
+
+    key0, query0, key1, query1 = [piece(vector_buf, i) for i in range(4)]
+    found0, found1, found2, found3 = [piece(found_buf, i) for i in range(4)]
+    strength0, strength1 = steps(strengths)
+    decay0, decay1 = steps(decays)
+    change0 = (value_buf[0, there] - decay0 * found0) * strength0
+    read0 = decay0 * found1 + inner(query0, key0) * change0
+    kept = decay0 * found2 + inner(key1, key0) * change0
+    change1 = (value_buf[1, there] - decay1 * kept) * strength1
+    kept = decay0 * found3 + inner(query1, key0) * change0
+    read1 = decay1 * kept + inner(query1, key1) * change1
+    for step, (read, gate) in enumerate(zip((read0, read1), steps(gates))):
+        scale = lax.rsqrt(jnp.mean(read * read, axis=-1, keepdims=True) + 1e-06)
+        start = (step * ROWS + first) * HEADS
+        normed_buf[start : start + CHUNK * HEADS, :] = (read * scale * gate).reshape(
+            CHUNK * HEADS, DV
+        )
+    for i, value in enumerate((key0, key1, decay1 * change0, change1, decay0 * decay1)):
+        update_buf[there, i * HEADS : (i + 1) * HEADS, :] = value
 
 
 def flatten_heads(normed_buf, normed_ref):
@@ -148,29 +144,27 @@
             store(h + i, (kept + added[:, i * DV : (i + 1) * DV]).astype(bf16))
 
 
-def write_group(index, update_ref, memory_ref, target_ref):
-    for i in range(GROUP):
-        row = index * GROUP + i
+def write_rows(rows, update_buf, memory, target_ref):
+    for row in rows:
 
         def store(h, value, row=row):
             target_ref[row, h * DK : (h + 1) * DK, :] = value
 
-        write_row(
-            update_ref[row], lambda h, row=row: memory_ref[row, h * DK : (h + 1) * DK, :], store
-        )
+        write_row(update_buf[row], lambda h, row=row: memory(row, h), store)
 
 
 def first_kernel(
     x, gain, tail_query, tail_key, tail_value, conv_query, conv_key, conv_value,
-    w_query, w_key, w_value, w_gate, w_beta, w_decay, decay_log, dt_bias, state,
-    late_query_ref, late_key_ref, late_value_ref, late_gate_ref, late_strength_ref, late_forget_ref,
-    raw_ref, stored_ref, conv_ref, normed_ref, update_ref,
+    w_query, w_key, w_value, w_gate, w_beta, w_decay, decay_log, dt_bias,
+    late_query_ref, late_key_ref, late_value_ref,
+    early_strength_ref, early_forget_ref, early_gate_ref,
+    late_strength_ref, late_forget_ref, late_gate_ref,
+    raw_ref, stored_ref, conv_ref, vector_ref, value_ref,
     x_buf, gain_buf, tail_query_buf, tail_key_buf, tail_value_buf,
     conv_query_buf, conv_key_buf, conv_value_buf,
-    query_buf, key_buf, value_weight_buf, gate_weight_buf, beta_buf, decay_buf, decay_ref, bias_ref, state_buf,
-    window_query, window_key, window_value, gate_all, strength_all, forget_all, stored_buf,
-    vector_buf, value_buf, found_buf, normed_buf,
-    small_sem, weight_sem, state_sem,
+    query_buf, key_buf, value_buf, gate_buf, beta_buf, decay_buf, decay_ref, bias_ref,
+    window_query, window_key, window_value, strength_all, forget_all, stored_buf,
+    small_sem, weight_sem,
 ):
     rows = x_buf.shape[0]
     small = [
@@ -199,8 +193,8 @@
         pieces = (
             (w_query, query_buf, DK),
             (w_key, key_buf, DK),
-            (w_value, value_weight_buf, 2 * DV),
-            (w_gate, gate_weight_buf, 2 * DV),
+            (w_value, value_buf, 2 * DV),
+            (w_gate, gate_buf, 2 * DV),
         )
         copies = []
         for i, (hbm, buf, width) in enumerate(pieces):
@@ -210,19 +204,12 @@
             )
         return copies
 
-    def load(row):
-        return pltpu.make_async_copy(state.at[row], state_buf.at[row], state_sem.at[row])
-
     def begin(j):
-        if j < KEYS:
-            for copy in weights(j):
-                copy.start()
-        elif j < KEYS + 2:
-            for row in range((j - KEYS) * ROWS // 2, (j - KEYS + 1) * ROWS // 2):
-                load(row).start()
-
-    begin(0)
-    begin(1)
+        for copy in weights(j):
+            copy.start()
+
+    for j in range(AHEAD):
+        begin(j)
 
     for copy in small:
         copy.wait()
@@ -233,9 +220,6 @@
         bias = jnp.where(head == h, bias_ref[h], bias)
     rate = -jnp.exp(rate)
     x_all = x_buf[...]
-
-    def spread(target, start, h, block):
-        target[pl.ds(start * HEADS + h, block.shape[0], stride=HEADS), :] = block
 
     across = (((1,), (1,)), ((), ()))
     beta = lax.dot_general(x_all, beta_buf[...], across, preferred_element_type=f32)
@@ -274,12 +258,14 @@
     for j in range(KEYS):
         for copy in weights(j):
             copy.wait()
-        begin(j + 2)
+        if j + AHEAD < KEYS:
+            begin(j + AHEAD)
         one, two = slice(j * DK, (j + 1) * DK), slice(2 * j * DV, 2 * (j + 1) * DV)
         query = dot(x_all, query_buf[:, one]).astype(bf16)
         key = dot(x_all, key_buf[:, one]).astype(bf16)
-        value = dot(x_all, value_weight_buf[:, two]).astype(bf16)
-        gate = dot(x_all, gate_weight_buf[:, two])
+        value = dot(x_all, value_buf[:, two]).astype(bf16)
+        gate = dot(x_all, gate_buf[:, two])
+        gate = gate * jax.nn.sigmoid(gate)
         raw_ref[:, j * DK : (j + 1) * DK] = query[2 * ROWS :]
         raw_ref[:, (KEYS + j) * DK : (KEYS + j + 1) * DK] = key[2 * ROWS :]
         raw_ref[:, 2 * (KEYS + j) * DK : 2 * (KEYS + j + 1) * DK] = value[2 * ROWS :]
@@ -287,7 +273,6 @@
         old_query = tail_query_buf[:, :, one].reshape(history, DK).astype(f32)
         old_key = tail_key_buf[:, :, one].reshape(history, DK).astype(f32)
         old_value = tail_value_buf[:, :, two].reshape(history, 2 * DV).astype(f32)
-        gate = gate * jax.nn.sigmoid(gate)
         keep(j, old_query, query)
         keep(KEYS + j, old_key, key)
         for i in range(2):
@@ -296,45 +281,36 @@
             place(window_key, h, old_key, key)
             place(window_value, h, old_value[:, half], value[:, half])
             keep(2 * KEYS + h, old_value[:, half], value[:, half])
-            spread(gate_all, 0, h, gate[:, half] * gain_buf[...])
+            scaled = gate[:, half] * gain_buf[...]
+            spread(early_gate_ref, 0, h, scaled[: 2 * ROWS])
+            spread(late_gate_ref, 0, h, scaled[2 * ROWS :])
 
     late = (history + 2 * ROWS) * HEADS
-    late_query_ref[...] = window_query[late:, :]
-    late_key_ref[...] = window_key[late:, :]
-    late_value_ref[...] = window_value[late:, :]
-    late_gate_ref[...] = gate_all[2 * ROWS * HEADS :, :]
-    late_strength_ref[...] = strength_all[2 * ROWS * HEADS :, :]
-    late_forget_ref[...] = forget_all[2 * ROWS * HEADS :, :]
+    late_query_ref[...] = window_query[late:, :].astype(bf16)
+    late_key_ref[...] = window_key[late:, :].astype(bf16)
+    late_value_ref[...] = window_value[late:, :].astype(bf16)
+    half = 2 * ROWS * HEADS
+    for value, early_ref, late_ref in (
+        (strength_all, early_strength_ref, late_strength_ref),
+        (forget_all, early_forget_ref, late_forget_ref),
+    ):
+        early_ref[...] = value[:half, :]
+        late_ref[...] = value[half:, :]
     stored_ref[...] = stored_buf[...].reshape(stored_ref.shape).astype(bf16)
-
     windows = (window_query, window_key, window_value)
     find_vectors(
         lambda kind, tap, first: part_of(windows[kind], tap, first, CHUNK),
         conv_ref,
-        vector_buf,
-        value_buf,
+        vector_ref,
+        value_ref,
     )
-    recall(
-        lambda row: load(row).wait(),
-        lambda row, h: state_buf[row, h * DK : (h + 1) * DK, :],
-        vector_buf,
-        found_buf,
-    )
-    finish(
-        lambda step, first: part_of(strength_all, step, first, CHUNK),
-        lambda step, first: part_of(forget_all, step, first, CHUNK),
-        lambda step, first: part_of(gate_all, step, first, CHUNK),
-        vector_buf,
-        value_buf,
-        found_buf,
-        normed_buf,
-        update_ref,
-    )
-    flatten_heads(normed_buf, normed_ref)
 
 
 def send_kernel(
-    wanted_ref, update_ref, tails_ref, state, slots, state_buf, stored_buf, state_sem, slot_sem
+    parent_ref, vector_ref, value_ref, strength_ref, forget_ref, gate_ref, tails_ref, state,
+    slots, normed_ref,
+    state_buf, stored_buf, found_buf, normed_buf, update_buf, wanted_buf, wanted_ref,
+    look_sem, state_sem, slot_sem,
 ):
     count = slots.shape[0]
 
@@ -343,49 +319,60 @@
 
     for row in range(ROWS):
         load(row).start()
+    parent = parent_ref[...]
+    mine = parent // ROWS == lax.axis_index("branch")
+    wanted = jnp.max(jnp.where(mine, parent % ROWS, -1).astype(f32), axis=-1, keepdims=True)
+    wanted_buf[...] = jnp.broadcast_to(wanted.astype(jnp.int32), wanted_buf.shape)
+    look = pltpu.make_async_copy(wanted_buf, wanted_ref, look_sem.at[0])
+    look.start()
+    for row in range(ROWS):
+        stored_buf[row, BODY:, :] = tails_ref[row]
 
     def ship(slot, row):
-        return (
-            pltpu.make_async_copy(
-                stored_buf.at[row], slots.at[slot, pl.ds(0, BODY)], slot_sem.at[0, slot]
-            ),
-            pltpu.make_async_copy(
-                tails_ref.at[row], slots.at[slot, pl.ds(BODY, SLOT - BODY)], slot_sem.at[1, slot]
-            ),
-        )
-
-    def group(index, carry):
-        for i in range(GROUP):
-            load(index * GROUP + i).wait()
-        write_group(index, update_ref, state_buf, stored_buf)
-
-        def begin(slot, carry):
+        return pltpu.make_async_copy(stored_buf.at[row], slots.at[slot], slot_sem.at[slot])
+
+    def memory(row, h):
+        return state_buf[row, h * DK : (h + 1) * DK, :]
+
+    for start in range(0, ROWS, SHIP):
+        rows = range(start, start + SHIP)
+        for row in rows:
+            load(row).wait()
+        recall(rows, memory, vector_ref, found_buf)
+        for first in range(start, start + SHIP, CHUNK):
+            finish(
+                first, strength_ref, forget_ref, gate_ref,
+                vector_ref, value_ref, found_buf, normed_buf, update_buf,
+            )
+        write_rows(rows, update_buf, memory, stored_buf)
+
+        if start == 0:
+            look.wait()
+
+        def begin(slot, carry, start=start):
             row = wanted_ref[slot, 0, 0]
 
-            @pl.when((row >= index * GROUP) & (row < (index + 1) * GROUP))
+            @pl.when((row >= start) & (row < start + SHIP))
             def _():
-                for copy in ship(slot, row):
-                    copy.start()
+                ship(slot, row).start()
 
             return carry
 
-        return lax.fori_loop(0, count, begin, carry)
-
-    lax.fori_loop(0, ROWS // GROUP, group, 0)
+        lax.fori_loop(0, count, begin, 0, unroll=4)
+    flatten_heads(normed_buf, normed_ref)
 
     def end(slot, carry):
         @pl.when(wanted_ref[slot, 0, 0] >= 0)
         def _():
-            for copy in ship(slot, 0):
-                copy.wait()
+            ship(slot, 0).wait()
 
         return carry
 
-    lax.fori_loop(0, count, end, 0)
+    lax.fori_loop(0, count, end, 0, unroll=4)
 
 
 def second_kernel(
-    slot_ref, late_query, late_key, late_value, late_gate, late_strength, late_forget, conv_ref, early_ref, slots, w_out,
+    parent_ref, late_query, late_key, late_value, late_strength, late_forget, late_gate, conv_ref, early_ref, slots, w_out,
     *refs,
 ):
     sums = refs[:PARTS]
@@ -397,12 +384,12 @@
     ) = refs[PARTS:]
     def load_tail(row):
         return pltpu.make_async_copy(
-            slots.at[slot_ref[row], pl.ds(BODY, SLOT - BODY)], tail_buf.at[row], tail_sem.at[row]
+            slots.at[parent_ref[row] // ROWS, pl.ds(BODY, SLOT - BODY)], tail_buf.at[row], tail_sem.at[row]
         )
 
     def load(row):
         return pltpu.make_async_copy(
-            slots.at[slot_ref[row], pl.ds(0, BODY)], memory_buf.at[row], memory_sem.at[row]
+            slots.at[parent_ref[row] // ROWS, pl.ds(0, BODY)], memory_buf.at[row], memory_sem.at[row]
         )
 
     for row in range(ROWS):
@@ -426,11 +413,11 @@
     for row in range(ROWS):
         tails = tail_buf[row]
         last_ref[row] = tails[2 * SLIM :]
-        spread = dot(wide, tails)
+        spaced = dot(wide, tails)
         for tap in range(TAPS - 1):
             for kind, window in enumerate((window_query, window_key, window_value)):
                 start = tap * WIDE + kind * HEADS
-                window[(tap * ROWS + row) * HEADS : (tap * ROWS + row + 1) * HEADS, :] = spread[
+                window[(tap * ROWS + row) * HEADS : (tap * ROWS + row + 1) * HEADS, :] = spaced[
                     start : start + HEADS
                 ]
     windows = (window_query, window_key, window_value)
@@ -439,32 +426,30 @@
     def window(kind, tap, first):
         if tap < TAPS - 1:
             return part_of(windows[kind], tap, first, CHUNK)
-        return part_of(fresh[kind], tap - (TAPS - 1), first, CHUNK)
+        return part_of(fresh[kind], tap - (TAPS - 1), first, CHUNK).astype(f32)
 
     find_vectors(window, conv_ref, vector_buf, value_buf)
-    recall(
-        lambda row: load(row).wait(),
-        lambda row, h: memory_buf[row, h * DK : (h + 1) * DK, :],
-        vector_buf,
-        found_buf,
-    )
-    finish(
-        lambda step, first: part_of(late_strength, step, first, CHUNK),
-        lambda step, first: part_of(late_forget, step, first, CHUNK),
-        lambda step, first: part_of(late_gate, step, first, CHUNK),
-        vector_buf,
-        value_buf,
-        found_buf,
-        normed_buf,
-        update_ref,
-    )
+
+    def group(index, carry):
+        rows = [index * GROUP + i for i in range(GROUP)]
+        for row in rows:
+            load(row).wait()
+        recall(rows, lambda row, h: memory_buf[row, h * DK : (h + 1) * DK, :], vector_buf, found_buf)
+        return carry
+
+    lax.fori_loop(0, ROWS // GROUP, group, 0)
+    for first in range(0, ROWS, CHUNK):
+        finish(
+            first, late_strength, late_forget, late_gate,
+            vector_buf, value_buf, found_buf, normed_buf, update_ref,
+        )
     normed_ref[: 2 * ROWS, :] = early_ref[...]
     flatten_heads(normed_buf, normed_ref.at[2 * ROWS :])
     for shift in range(PARTS):
         load_out(shift).wait()
     normed = normed_ref[...]
     for shift in range(PARTS):
-        sums[shift][...] = dot(normed, out_buf[shift])
+        sums[shift][...] = dot(normed, out_buf[shift]).astype(sums[shift].dtype)
 
 
 def final_kernel(
@@ -487,9 +472,12 @@
         start += width
 
     def group(index, carry):
-        write_group(index, update_ref, memory_ref, final_buf)
-        for i in range(GROUP):
-            save(index * GROUP + i).start()
+        rows = [index * GROUP + i for i in range(GROUP)]
+        write_rows(
+            rows, update_ref, lambda row, h: memory_ref[row, h * DK : (h + 1) * DK, :], final_buf
+        )
+        for row in rows:
+            save(row).start()
         return carry
 
     lax.fori_loop(0, ROWS // GROUP, group, 0)
@@ -524,62 +512,70 @@
     ]
 
 
-def first_half(arrays, state):
+def first_half(arrays):
     rows = arrays[0].shape[0]
-    late = rows // 2
+    half = rows // 2
     window = pltpu.VMEM(((TAPS - 1) * ROWS * HEADS + rows * HEADS, DV), f32)
     wide = pltpu.VMEM((rows * HEADS, DV), f32)
     return pl.pallas_call(
         first_kernel,
-        in_specs=[HBM] * (len(arrays) + 1),
-        out_specs=[VMEM] * 11,
+        in_specs=[HBM] * len(arrays),
+        out_specs=[VMEM] * 14,
         out_shape=(
-            *[shape((late * HEADS, DV), f32)] * 6,
-            shape((late, SLIM * DV), bf16),
+            *[shape((half * HEADS, DV), bf16)] * 3,
+            *[shape((half * HEADS, DV), f32)] * 6,
+            shape((half, SLIM * DV), bf16),
             shape((ROWS, (TAPS - 1) * SLIM, DV), bf16),
             shape((3, TAPS, HEADS, DV), f32),
-            shape((late, HEADS * DV), bf16),
-            shape((ROWS, 5 * HEADS, DV), f32),
+            shape((ROWS, 4 * HEADS, DV), f32),
+            shape((2, ROWS, HEADS, DV), f32),
         ),
         scratch_shapes=[
             *[buffer(array) for array in arrays[:-2]],
             *[pltpu.SMEM(array.shape, f32) for array in arrays[-2:]],
-            buffer(state),
             window,
             window,
             window,
             wide,
             wide,
-            wide,
             pltpu.VMEM((ROWS * (TAPS - 1) * SLIM, DV), f32),
-            *work_buffers(),
-            pltpu.SemaphoreType.DMA((12,)),
+            pltpu.SemaphoreType.DMA((len(arrays) - 4,)),
             pltpu.SemaphoreType.DMA((4 * KEYS,)),
-            pltpu.SemaphoreType.DMA((ROWS,)),
         ],
         compiler_params=PARAMS,
         name="first_half",
-    )(*[in_hbm(array) for array in arrays], in_hbm(state))
-
-
-def fill_slots(wanted, update, tails, state):
+    )(*[in_hbm(array) for array in arrays])
+
+
+def fill_slots(parents, early, tails, state):
+    count = parents.shape[0]
+    _, _, found, normed = work_buffers()
     return pl.pallas_call(
         send_kernel,
-        in_specs=[SMEM, VMEM, VMEM, HBM],
-        out_specs=HBM,
-        out_shape=shape((wanted.shape[0], SLOT, DV), bf16),
+        in_specs=[VMEM] * 7 + [HBM],
+        out_specs=[HBM, VMEM],
+        out_shape=(
+            shape((count, SLOT, DV), bf16),
+            shape((2 * ROWS, HEADS * DV), bf16),
+        ),
         scratch_shapes=[
             buffer(state),
-            buffer(state),
+            pltpu.VMEM((ROWS, SLOT, DV), bf16),
+            found,
+            normed,
+            pltpu.VMEM((ROWS, 5 * HEADS, DV), f32),
+            pltpu.VMEM((count, 1, DV), jnp.int32),
+            pltpu.SMEM((count, 1, DV), jnp.int32),
+            pltpu.SemaphoreType.DMA((1,)),
             pltpu.SemaphoreType.DMA((ROWS,)),
-            pltpu.SemaphoreType.DMA((2, wanted.shape[0])),
+            pltpu.SemaphoreType.DMA((count,)),
         ],
         compiler_params=PARAMS,
         name="fill_slots",
-    )(wanted, update, tails, in_hbm(state))
-
-
-def second_half(slot_of_row, late, conv, normed, slots, w_out):
+    )(parents, *early, tails, in_hbm(state))
+
+
+def second_half(parents, late, conv, normed, slots, w_out):
     window = pltpu.VMEM(((TAPS - 1) * ROWS * HEADS, DV), f32)
     rows, width = 2 * normed.shape[0], w_out.shape[1] // PARTS
     *sums, update, last, memory = pl.pallas_call(
@@ -587,7 +583,8 @@
         in_specs=[SMEM] + [VMEM] * 8 + [HBM] * 2,
         out_specs=[VMEM] * (PARTS + 3),
         out_shape=(
-            *[shape((rows, width), f32)] * PARTS,
+            shape((rows, width), f32),
+            *[shape((rows, width), bf16)] * (PARTS - 1),
             shape((ROWS, 5 * HEADS, DV), f32),
             shape((ROWS, SLIM, DV), bf16),
             shape((ROWS, BODY, DV), bf16),
@@ -606,7 +603,7 @@
         ],
         compiler_params=PARAMS,
         name="second_half",
-    )(slot_of_row, *late, conv, normed, in_hbm(slots), in_hbm(w_out))
+    )(parents, *late, conv, normed, in_hbm(slots), in_hbm(w_out))
     return sums, update, last, memory
 
 
@@ -633,9 +630,9 @@
 
 def sum_heads(blocks):
     total = blocks[0]
-    for shift in range(1, PARTS):
+    for shift in (1, 3, 2):
         pairs = [(i, (i + shift) % PARTS) for i in range(PARTS)]
-        total = total + lax.ppermute(blocks[shift], "tensor", pairs)
+        total = total + lax.ppermute(blocks[shift], "tensor", pairs).astype(f32)
     return total.astype(bf16)
 
 
@@ -661,15 +658,13 @@
     parents,
 ):
     groups = lax.axis_size("branch")
-    source, offset = parents // ROWS, parents % ROWS
-    hits = source[:, None] == jnp.arange(groups, dtype=jnp.int32)[None, :]
-    wanted = jnp.sum(jnp.where(hits, offset[:, None] + 1, 0), axis=0) - 1
-    requested = lax.all_to_all(
-        wanted.reshape(groups, 1, 1), "branch", split_axis=0, concat_axis=0, tiled=True
-    )
+    asked = jnp.broadcast_to(parents[None, None, :], (groups, 1, ROWS))
+    asked = lax.all_to_all(asked, "branch", split_axis=0, concat_axis=0, tiled=True)
 
     flat_state = state.reshape(ROWS, BODY, DV)
-    *late, raw, stored_tails, conv, normed, update = first_half(
+    (
+        late_query, late_key, late_value, *scales, raw, stored_tails, conv, vectors, values
+    ) = first_half(
         (
             inputs.reshape(-1, inputs.shape[-1]),
             norm_gain[None],
@@ -687,13 +682,14 @@
             w_decay.T,
             decay_log,
             dt_bias,
-        ),
-        flat_state,
+        )
     )
-    shipped = fill_slots(requested, update, stored_tails, flat_state)
+    shipped, normed = fill_slots(asked, (vectors, values, *scales[:3]), stored_tails, flat_state)
     arrived = lax.all_to_all(shipped, "branch", split_axis=0, concat_axis=0, tiled=True)
-
-    sums, update, last, memory = second_half(source, late, conv, normed, arrived, w_out)
+    late = (late_query, late_key, late_value, *scales[3:])
+    sums, update, last, memory = second_half(
+        parents, late, conv, normed, arrived, w_out
+    )
     out_rows = sum_heads(sums).reshape(inputs.shape[0], ROWS, -1)
     final_state, *final_tails = last_memory(update, last, raw, memory)
     return (

time: 152 us -> 147 us (0.967)
  Pallas kernels: 25.7 us -> 22.6 us
    pallas_call x2, Pallas kernels: 15.4 us -> 12.7 us  [the longest x1 6.98 us: first_half(): pl.pallas_call(first_kernel, in_specs=[HBM] * len(arrays), out_specs=[VME...]
  transfers between devices with their start and end apart: 4 -> 4, of which waited for: 1 -> 2; matrix products, arithmetic and copies ran while one was open for 0% -> 0% of each run, Pallas kernels for 8% -> 7%
where the time goes in v3:
time: 147 us
  blocking collectives  107 us (73%)
  Pallas kernels  22.6 us (15%)
  starting transfers between devices  13.5 us (9%)
    all_to_all x1, blocking collectives, per_device(): lax.all_to_all(shipped, 'branch', split_axis=0, concat_axis=0, tiled=True)  107 us
    all_to_all x1, starting transfers between devices, per_device(): lax.all_to_all(asked, 'branch', split_axis=0, concat_axis=0, tiled=True)  8.24 us
    pallas_call x1, Pallas kernels, first_half(): pl.pallas_call(first_kernel, in_specs=[HBM] * len(arrays), out_specs=[VME...  6.98 us
    pallas_call x1, Pallas kernels, second_half(): pl.pallas_call(second_kernel, in_specs=[SMEM] + [VMEM] * 8 + [HBM] * 2, o...  6.22 us
    pallas_call x1, Pallas kernels, fill_slots(): pl.pallas_call(send_kernel, in_specs=[VMEM] * 7 + [HBM], out_specs=[HBM,...  5.71 us
    ppermute x3, starting transfers between devices, sum_heads(): total = total + lax.ppermute(blocks[shift], 'tensor', pairs).astype(f32)  5.29 us
    pallas_call x1, Pallas kernels, last_memory(): pl.pallas_call(final_kernel, in_specs=[VMEM] * 4, out_specs=[HBM] + [VMEM...  3.69 us
  transfers between devices with their start and end apart: 4, of which 2 were waited for; matrix products, arithmetic and copies ran while one was open for 0% of the time, Pallas kernels for 7%

profile of v3, /device:TPU:0, one launch (start us, length us, event | category | flops | bytes accessed | tf_op | source)
XLA Modules:
  0.0 146.5 jit_solution(16796108648744767798)
XLA Ops:
  0.6 1.3 broadcast_in_dim.10
  1.9 8.2 %all-to-all-start = ((s32[32,1,16]{2,1,0:T(1,128)}), s32[32,1,16]{2,1,0:T(1,128)S(1)}, u32[]{:S(2)}, u32[]{:S(2)}) async-start(s32[32,1,16]{2,1,0:T(1,128)} %broadcast_in_dim.10), calls=%async_computation | async-start | bytes 32768 | tf_op jit(solution)/shard_map/all_to_all | solution.py:662
  10.2 7.0 %first_half.1 = (bf16[256,128]{1,0:T(8,128)(2,1)S(1)}, bf16[256,128]{1,0:T(8,128)(2,1)S(1)}, bf16[256,128]{1,0:T(8,128)(2,1)S(1)}, f32[256,128]{1,0:T(8,128)S(1)...) custom-call(bf16[64,2048]{1,0:T(8,128)(2,1)} %bitcast.14, ...), custom_call_target="tpu_custom_call" | custom-call | tf_op jit(solution)/shard_map/first_half/pallas_call | solution.py:520
  17.1 0.3 all-to-all-done.parent_ref
  17.4 5.7 %fill_slots.1 = (bf16[32,1072,128]{2,1,0:T(8,128)(2,1)}, bf16[32,1024]{1,0:T(8,128)(2,1)S(1)}) custom-call(s32[32,1,16]{2,1,0:T(1,128)S(1)} %all-to-all-done.parent_ref, f32[16,32,128]{2,1,0:T(8,128)S(1)} %get-tuple-element.39.vector_ref, f32[2,16,8,128]{3,2,1,0:T(8,128)S(1)} %get-tuple-element.40.value_ref, f32[256,128]{1,0:T(8,128)S(1)} %get-tuple-element.41.strength_ref, ...), custom_call_target="tpu_custom_call" | custom-call | tf_op jit(solution)/shard_map/fill_slots/pallas_call | solution.py:553
  23.2 0.0 copy-start
  23.2 107.4 %all_to_all.10.slots = bf16[32,1072,128]{2,1,0:T(8,128)(2,1)} all-to-all(bf16[32,1072,128]{2,1,0:T(8,128)(2,1)} %get-tuple-element.46), channel_id=1, replica_groups=mesh['branch'=32,'tensor'=4] {'branch'}, dimensions={0} | all-to-all | bytes 17563648 | tf_op jit(solution)/shard_map/all_to_all | solution.py:688
  130.5 0.0 copy-done
  130.5 6.2 %second_half.1 = (f32[64,512]{1,0:T(8,128)S(1)}, bf16[64,512]{1,0:T(8,128)(2,1)S(1)}, bf16[64,512]{1,0:T(8,128)(2,1)S(1)}, bf16[64,512]{1,0:T(8,128)(2,1)S(1)}, ...) custom-call(s32[16]{0:T(128)S(1)} %copy-done, ...), custom_call_target="tpu_custom_call" | custom-call | tf_op jit(solution)/shard_map/second_half/pallas_call | solution.py:581
  136.8 1.7 %collective-permute-start = (bf16[64,512]{1,0:T(8,128)(2,1)S(1)}, bf16[64,512]{1,0:T(8,128)(2,1)S(1)}, u32[]{:S(2)}, u32[]{:S(2)}) collective-permute-start(bf16[64,512]{1,0:T(8,128)(2,1)S(1)} %get-tuple-element.48), channel_id=1, source_target_pairs={{0,1},{1,2},{2,3},{3,0},{4,5},{5,6},{6,7},{7,4},{8,9},{9,10},{10,1... | collective-permute-start | bytes 196616 | tf_op jit(solution)/shard_map/ppermute | solution.py:635
  138.4 1.7 %collective-permute-start.1 = (bf16[64,512]{1,0:T(8,128)(2,1)S(1)}, bf16[64,512]{1,0:T(8,128)(2,1)S(1)}, u32[]{:S(2)}, u32[]{:S(2)}) collective-permute-start(bf16[64,512]{1,0:T(8,128)(2,1)S(1)} %get-tuple-element.49), channel_id=1, source_target_pairs={{0,3},{1,0},{2,1},{3,2},{4,7},{5,4},{6,5},{7,6},{8,11},{9,8},{10,9... | collective-permute-start | bytes 196616 | tf_op jit(solution)/shard_map/ppermute | solution.py:635
  140.1 2.0 %collective-permute-start.2 = (bf16[64,512]{1,0:T(8,128)(2,1)S(1)}, bf16[64,512]{1,0:T(8,128)(2,1)S(1)}, u32[]{:S(2)}, u32[]{:S(2)}) collective-permute-start(bf16[64,512]{1,0:T(8,128)(2,1)S(1)} %get-tuple-element.50), channel_id=1, source_target_pairs={{0,2},{1,3},{2,0},{3,1},{4,6},{5,7},{6,4},{7,5},{8,10},{9,11},{10,... | collective-permute-start | bytes 196616 | tf_op jit(solution)/shard_map/ppermute | solution.py:635
  142.1 3.7 %last_memory.1 = (bf16[16,1024,128]{2,1,0:T(8,128)(2,1)}, bf16[3,16,512]{2,1,0:T(8,128)(2,1)}, bf16[3,16,512]{2,1,0:T(8,128)(2,1)}, bf16[3,16,1024]{2,1,0:T(8,128)(2,1)}) custom-call(f32[16,40,128]{2,1,0:T(8,128)S(1)} %get-tuple-element.51.update_ref, bf16[16,16,128]{2,1,0:T(8,128)(2,1)S(1)} %get-tuple-element.52.last_ref, ...), custom_call_target="tpu_custom_call" | custom-call | tf_op jit(solution)/shard_map/last_memory/pallas_call | solution.py:611
  145.8 0.0 collective-permute-done
  145.8 0.0 collective-permute-done.1
  145.8 0.1 collective-permute-done.2
  145.8 0.7 add_convert_fusion
Async XLA Ops:
  1.9 15.5 %all-to-all-start = ((s32[32,1,16]{2,1,0:T(1,128)}), s32[32,1,16]{2,1,0:T(1,128)S(1)}, u32[]{:S(2)}, u32[]{:S(2)}) async-start(s32[32,1,16]{2,1,0:T(1,128)} %broadcast_in_dim.10), calls=%async_computation | async-start | bytes 32768 | tf_op jit(solution)/shard_map/all_to_all | solution.py:662
  23.2 107.4 %copy-start = (s32[16]{0:T(128)S(1)}, s32[16]{0:T(128)}, u32[]{:S(2)}) copy-start(s32[16]{0:T(128)} %parent_ref.1) | copy-start | bytes 196
  136.8 9.0 %collective-permute-start = (bf16[64,512]{1,0:T(8,128)(2,1)S(1)}, bf16[64,512]{1,0:T(8,128)(2,1)S(1)}, u32[]{:S(2)}, u32[]{:S(2)}) collective-permute-start(bf16[64,512]{1,0:T(8,128)(2,1)S(1)} %get-tuple-element.48), channel_id=1, source_target_pairs={{0,1},{1,2},{2,3},{3,0},{4,5},{5,6},{6,7},{7,4},{8,9},{9,10},{10,1... | collective-permute-start | bytes 196616 | tf_op jit(solution)/shard_map/ppermute | solution.py:635
  138.4 7.4 %collective-permute-start.1 = (bf16[64,512]{1,0:T(8,128)(2,1)S(1)}, bf16[64,512]{1,0:T(8,128)(2,1)S(1)}, u32[]{:S(2)}, u32[]{:S(2)}) collective-permute-start(bf16[64,512]{1,0:T(8,128)(2,1)S(1)} %get-tuple-element.49), channel_id=1, source_target_pairs={{0,3},{1,0},{2,1},{3,2},{4,7},{5,4},{6,5},{7,6},{8,11},{9,8},{10,9... | collective-permute-start | bytes 196616 | tf_op jit(solution)/shard_map/ppermute | solution.py:635
  140.1 5.8 %collective-permute-start.2 = (bf16[64,512]{1,0:T(8,128)(2,1)S(1)}, bf16[64,512]{1,0:T(8,128)(2,1)S(1)}, u32[]{:S(2)}, u32[]{:S(2)}) collective-permute-start(bf16[64,512]{1,0:T(8,128)(2,1)S(1)} %get-tuple-element.50), channel_id=1, source_target_pairs={{0,2},{1,3},{2,0},{3,1},{4,6},{5,7},{6,4},{7,5},{8,10},{9,11},{10,... | collective-permute-start | bytes 196616 | tf_op jit(solution)/shard_map/ppermute | solution.py:635

commit v4 on v3

--- a/solution.py
+++ b/solution.py
@@ -19,6 +19,7 @@
 CHUNK = 4
 PARTS = 4
 GROUP = 8
+LATE = 16
 AHEAD = 2
 SHIP = 8
 f32 = jnp.float32
@@ -431,13 +432,13 @@
     find_vectors(window, conv_ref, vector_buf, value_buf)
 
     def group(index, carry):
-        rows = [index * GROUP + i for i in range(GROUP)]
+        rows = [index * LATE + i for i in range(LATE)]
         for row in rows:
             load(row).wait()
         recall(rows, lambda row, h: memory_buf[row, h * DK : (h + 1) * DK, :], vector_buf, found_buf)
         return carry
 
-    lax.fori_loop(0, ROWS // GROUP, group, 0)
+    lax.fori_loop(0, ROWS // LATE, group, 0)
     for first in range(0, ROWS, CHUNK):
         finish(
             first, late_strength, late_forget, late_gate,
@@ -454,15 +455,16 @@
 
 def final_kernel(
     update_ref, last_ref, raw_ref, memory_ref,
-    final, query_ref, key_ref, value_ref,
-    final_buf, last_buf, final_sem,
+    final, query, key, value,
+    final_buf, last_buf, query_buf, key_buf, value_buf, final_sem, tail_sem,
 ):
     def save(row):
         return pltpu.make_async_copy(final_buf.at[row], final.at[row], final_sem.at[row])
 
     start = 0
     last_buf[...] = last_ref[...].astype(f32).reshape(ROWS * SLIM, DV)
-    for ref in (query_ref, key_ref, value_ref):
+    tails = []
+    for i, (ref, target) in enumerate(((query_buf, query), (key_buf, key), (value_buf, value))):
         width = ref.shape[2]
         for channel in range(width // DV):
             block = last_buf[pl.ds(start // DV + channel, ROWS, stride=SLIM), :]
@@ -470,6 +472,8 @@
         for step in range(2):
             ref[1 + step] = raw_ref[step * ROWS : (step + 1) * ROWS, start : start + width]
         start += width
+        tails.append(pltpu.make_async_copy(ref, target, tail_sem.at[i]))
+        tails[i].start()
 
     def group(index, carry):
         rows = [index * GROUP + i for i in range(GROUP)]
@@ -481,6 +485,8 @@
         return carry
 
     lax.fori_loop(0, ROWS // GROUP, group, 0)
+    for copy in tails:
+        copy.wait()
     for row in range(ROWS):
         save(row).wait()
 
@@ -608,20 +614,18 @@
 
 
 def last_memory(update, last, raw, memory):
+    tails = [shape((TAPS - 1, ROWS, width), bf16) for width in (KEYS * DK, KEYS * DK, HEADS * DV)]
     return pl.pallas_call(
         final_kernel,
         in_specs=[VMEM] * 4,
-        out_specs=[HBM] + [VMEM] * 3,
-        out_shape=(
-            shape((ROWS, BODY, DV), bf16),
-            shape((TAPS - 1, ROWS, KEYS * DK), bf16),
-            shape((TAPS - 1, ROWS, KEYS * DK), bf16),
-            shape((TAPS - 1, ROWS, HEADS * DV), bf16),
-        ),
+        out_specs=[HBM] * 4,
+        out_shape=(shape((ROWS, BODY, DV), bf16), *tails),
         scratch_shapes=[
             buffer(memory),
             pltpu.VMEM((ROWS * SLIM, DV), f32),
+            *[buffer(tail) for tail in tails],
             pltpu.SemaphoreType.DMA((ROWS,)),
+            pltpu.SemaphoreType.DMA((3,)),
         ],
         compiler_params=PARAMS,
         name="last_memory",

time: 147 us -> 147 us (level)
  no operation moved by 1% of the time
where the time goes in v4:
time: 147 us; the launch traced here: 146 us
  blocking collectives  108 us (73%)
  Pallas kernels  21.5 us (15%)
  starting transfers between devices  13.6 us (9%)
    all_to_all x1, blocking collectives, per_device(): lax.all_to_all(shipped, 'branch', split_axis=0, concat_axis=0, tiled=True)  108 us
    all_to_all x1, starting transfers between devices, per_device(): lax.all_to_all(asked, 'branch', split_axis=0, concat_axis=0, tiled=True)  8.24 us
    pallas_call x1, Pallas kernels, first_half(): pl.pallas_call(first_kernel, in_specs=[HBM] * len(arrays), out_specs=[VME...  6.98 us
    pallas_call x1, Pallas kernels, second_half(): pl.pallas_call(second_kernel, in_specs=[SMEM] + [VMEM] * 8 + [HBM] * 2, o...  5.95 us
    pallas_call x1, Pallas kernels, fill_slots(): pl.pallas_call(send_kernel, in_specs=[VMEM] * 7 + [HBM], out_specs=[HBM,...  5.5 us
    ppermute x3, starting transfers between devices, sum_heads(): total = total + lax.ppermute(blocks[shift], 'tensor', pairs).astype(f32)  5.38 us
    pallas_call x1, Pallas kernels, last_memory(): pl.pallas_call(final_kernel, in_specs=[VMEM] * 4, out_specs=[HBM] * 4, ou...  3.06 us
  transfers between devices with their start and end apart: 4, of which 2 were waited for; matrix products, arithmetic and copies ran while one was open for 0% of the time, Pallas kernels for 7%

profile of v4, /device:TPU:0, one launch (start us, length us, event | category | flops | bytes accessed | tf_op | source)
XLA Modules:
  0.0 146.2 jit_solution(6272301762778034490)
XLA Ops:
  0.6 1.3 broadcast_in_dim.10
  1.9 8.2 %all-to-all-start = ((s32[32,1,16]{2,1,0:T(1,128)}), s32[32,1,16]{2,1,0:T(1,128)S(1)}, u32[]{:S(2)}, u32[]{:S(2)}) async-start(s32[32,1,16]{2,1,0:T(1,128)} %broadcast_in_dim.10), calls=%async_computation | async-start | bytes 32768 | tf_op jit(solution)/shard_map/all_to_all | solution.py:666
  10.2 7.0 %first_half.1 = (bf16[256,128]{1,0:T(8,128)(2,1)S(1)}, bf16[256,128]{1,0:T(8,128)(2,1)S(1)}, bf16[256,128]{1,0:T(8,128)(2,1)S(1)}, f32[256,128]{1,0:T(8,128)S(1)...) custom-call(bf16[64,2048]{1,0:T(8,128)(2,1)} %bitcast.14, ...), custom_call_target="tpu_custom_call" | custom-call | tf_op jit(solution)/shard_map/first_half/pallas_call | solution.py:526
  17.1 0.3 all-to-all-done.parent_ref
  17.4 5.5 %fill_slots.1 = (bf16[32,1072,128]{2,1,0:T(8,128)(2,1)}, bf16[32,1024]{1,0:T(8,128)(2,1)S(1)}) custom-call(s32[32,1,16]{2,1,0:T(1,128)S(1)} %all-to-all-done.parent_ref, f32[16,32,128]{2,1,0:T(8,128)S(1)} %get-tuple-element.39.vector_ref, f32[2,16,8,128]{3,2,1,0:T(8,128)S(1)} %get-tuple-element.40.value_ref, f32[256,128]{1,0:T(8,128)S(1)} %get-tuple-element.41.strength_ref, ...), custom_call_target="tpu_custom_call" | custom-call | tf_op jit(solution)/shard_map/fill_slots/pallas_call | solution.py:559
  22.9 0.0 copy-start
  23.0 107.6 %all_to_all.10.slots = bf16[32,1072,128]{2,1,0:T(8,128)(2,1)} all-to-all(bf16[32,1072,128]{2,1,0:T(8,128)(2,1)} %get-tuple-element.46), channel_id=1, replica_groups=mesh['branch'=32,'tensor'=4] {'branch'}, dimensions={0} | all-to-all | bytes 17563648 | tf_op jit(solution)/shard_map/all_to_all | solution.py:692
  130.5 0.0 copy-done
  130.5 6.0 %second_half.1 = (f32[64,512]{1,0:T(8,128)S(1)}, bf16[64,512]{1,0:T(8,128)(2,1)S(1)}, bf16[64,512]{1,0:T(8,128)(2,1)S(1)}, bf16[64,512]{1,0:T(8,128)(2,1)S(1)}, ...) custom-call(s32[16]{0:T(128)S(1)} %copy-done, ...), custom_call_target="tpu_custom_call" | custom-call | tf_op jit(solution)/shard_map/second_half/pallas_call | solution.py:587
  136.5 1.6 %collective-permute-start = (bf16[64,512]{1,0:T(8,128)(2,1)S(1)}, bf16[64,512]{1,0:T(8,128)(2,1)S(1)}, u32[]{:S(2)}, u32[]{:S(2)}) collective-permute-start(bf16[64,512]{1,0:T(8,128)(2,1)S(1)} %get-tuple-element.48), channel_id=1, source_target_pairs={{0,1},{1,2},{2,3},{3,0},{4,5},{5,6},{6,7},{7,4},{8,9},{9,10},{10,1... | collective-permute-start | bytes 196616 | tf_op jit(solution)/shard_map/ppermute | solution.py:639
  138.1 1.7 %collective-permute-start.1 = (bf16[64,512]{1,0:T(8,128)(2,1)S(1)}, bf16[64,512]{1,0:T(8,128)(2,1)S(1)}, u32[]{:S(2)}, u32[]{:S(2)}) collective-permute-start(bf16[64,512]{1,0:T(8,128)(2,1)S(1)} %get-tuple-element.49), channel_id=1, source_target_pairs={{0,3},{1,0},{2,1},{3,2},{4,7},{5,4},{6,5},{7,6},{8,11},{9,8},{10,9... | collective-permute-start | bytes 196616 | tf_op jit(solution)/shard_map/ppermute | solution.py:639
  139.8 2.1 %collective-permute-start.2 = (bf16[64,512]{1,0:T(8,128)(2,1)S(1)}, bf16[64,512]{1,0:T(8,128)(2,1)S(1)}, u32[]{:S(2)}, u32[]{:S(2)}) collective-permute-start(bf16[64,512]{1,0:T(8,128)(2,1)S(1)} %get-tuple-element.50), channel_id=1, source_target_pairs={{0,2},{1,3},{2,0},{3,1},{4,6},{5,7},{6,4},{7,5},{8,10},{9,11},{10,... | collective-permute-start | bytes 196616 | tf_op jit(solution)/shard_map/ppermute | solution.py:639
  141.9 3.1 %last_memory.1 = (bf16[16,1024,128]{2,1,0:T(8,128)(2,1)}, bf16[3,16,512]{2,1,0:T(8,128)(2,1)}, bf16[3,16,512]{2,1,0:T(8,128)(2,1)}, bf16[3,16,1024]{2,1,0:T(8,128)(2,1)}) custom-call(f32[16,40,128]{2,1,0:T(8,128)S(1)} %get-tuple-element.51.update_ref, bf16[16,16,128]{2,1,0:T(8,128)(2,1)S(1)} %get-tuple-element.52.last_ref, ...), custom_call_target="tpu_custom_call" | custom-call | tf_op jit(solution)/shard_map/last_memory/pallas_call | solution.py:618
  144.9 0.0 collective-permute-done
  144.9 0.0 collective-permute-done.1
  145.0 0.6 collective-permute-done.2
  145.6 0.7 add_convert_fusion
Async XLA Ops:
  1.9 15.5 %all-to-all-start = ((s32[32,1,16]{2,1,0:T(1,128)}), s32[32,1,16]{2,1,0:T(1,128)S(1)}, u32[]{:S(2)}, u32[]{:S(2)}) async-start(s32[32,1,16]{2,1,0:T(1,128)} %broadcast_in_dim.10), calls=%async_computation | async-start | bytes 32768 | tf_op jit(solution)/shard_map/all_to_all | solution.py:666
  22.9 107.6 %copy-start = (s32[16]{0:T(128)S(1)}, s32[16]{0:T(128)}, u32[]{:S(2)}) copy-start(s32[16]{0:T(128)} %parent_ref.1) | copy-start | bytes 196
  136.5 8.4 %collective-permute-start = (bf16[64,512]{1,0:T(8,128)(2,1)S(1)}, bf16[64,512]{1,0:T(8,128)(2,1)S(1)}, u32[]{:S(2)}, u32[]{:S(2)}) collective-permute-start(bf16[64,512]{1,0:T(8,128)(2,1)S(1)} %get-tuple-element.48), channel_id=1, source_target_pairs={{0,1},{1,2},{2,3},{3,0},{4,5},{5,6},{6,7},{7,4},{8,9},{9,10},{10,1... | collective-permute-start | bytes 196616 | tf_op jit(solution)/shard_map/ppermute | solution.py:639
  138.1 6.8 %collective-permute-start.1 = (bf16[64,512]{1,0:T(8,128)(2,1)S(1)}, bf16[64,512]{1,0:T(8,128)(2,1)S(1)}, u32[]{:S(2)}, u32[]{:S(2)}) collective-permute-start(bf16[64,512]{1,0:T(8,128)(2,1)S(1)} %get-tuple-element.49), channel_id=1, source_target_pairs={{0,3},{1,0},{2,1},{3,2},{4,7},{5,4},{6,5},{7,6},{8,11},{9,8},{10,9... | collective-permute-start | bytes 196616 | tf_op jit(solution)/shard_map/ppermute | solution.py:639
  139.8 5.8 %collective-permute-start.2 = (bf16[64,512]{1,0:T(8,128)(2,1)S(1)}, bf16[64,512]{1,0:T(8,128)(2,1)S(1)}, u32[]{:S(2)}, u32[]{:S(2)}) collective-permute-start(bf16[64,512]{1,0:T(8,128)(2,1)S(1)} %get-tuple-element.50), channel_id=1, source_target_pairs={{0,2},{1,3},{2,0},{3,1},{4,6},{5,7},{6,4},{7,5},{8,10},{9,11},{10,... | collective-permute-start | bytes 196616 | tf_op jit(solution)/shard_map/ppermute | solution.py:639

commit v5 on v4

--- a/solution.py
+++ b/solution.py
@@ -92,7 +92,7 @@
         found_buf[row] = jnp.concatenate(found, axis=0)
 
 
-def finish(first, strengths, decays, gates, vector_buf, value_buf, found_buf, normed_buf, update_buf):
+def finish(first, strengths, decays, vector_buf, value_buf, found_buf, normed_buf, update_buf):
     there = slice(first, first + CHUNK)
 
     def piece(ref, i):
@@ -111,20 +111,19 @@
     change1 = (value_buf[1, there] - decay1 * kept) * strength1
     kept = decay0 * found3 + inner(query1, key0) * change0
     read1 = decay1 * kept + inner(query1, key1) * change1
-    for step, (read, gate) in enumerate(zip((read0, read1), steps(gates))):
+    for step, read in enumerate((read0, read1)):
         scale = lax.rsqrt(jnp.mean(read * read, axis=-1, keepdims=True) + 1e-06)
         start = (step * ROWS + first) * HEADS
-        normed_buf[start : start + CHUNK * HEADS, :] = (read * scale * gate).reshape(
-            CHUNK * HEADS, DV
-        )
+        normed_buf[start : start + CHUNK * HEADS, :] = (read * scale).reshape(CHUNK * HEADS, DV)
     for i, value in enumerate((key0, key1, decay1 * change0, change1, decay0 * decay1)):
         update_buf[there, i * HEADS : (i + 1) * HEADS, :] = value
 
 
-def flatten_heads(normed_buf, normed_ref):
+def flatten_heads(normed_buf, gate_buf, first, normed_ref):
     for h in range(HEADS):
-        rows = normed_buf[pl.ds(h, 2 * ROWS, stride=HEADS), :]
-        normed_ref[:, h * DV : (h + 1) * DV] = rows.astype(bf16)
+        normed = normed_buf[pl.ds(h, 2 * ROWS, stride=HEADS), :]
+        gate = gate_buf[pl.ds(first * HEADS + h, 2 * ROWS, stride=HEADS), :]
+        normed_ref[first : first + 2 * ROWS, h * DV : (h + 1) * DV] = (normed * gate).astype(bf16)
 
 
 def write_row(update, memory, store):
@@ -158,9 +157,8 @@
     x, gain, tail_query, tail_key, tail_value, conv_query, conv_key, conv_value,
     w_query, w_key, w_value, w_gate, w_beta, w_decay, decay_log, dt_bias,
     late_query_ref, late_key_ref, late_value_ref,
-    early_strength_ref, early_forget_ref, early_gate_ref,
-    late_strength_ref, late_forget_ref, late_gate_ref,
-    raw_ref, stored_ref, conv_ref, vector_ref, value_ref,
+    early_strength_ref, early_forget_ref, late_strength_ref, late_forget_ref,
+    gate_ref, raw_ref, stored_ref, conv_ref, vector_ref, value_ref,
     x_buf, gain_buf, tail_query_buf, tail_key_buf, tail_value_buf,
     conv_query_buf, conv_key_buf, conv_value_buf,
     query_buf, key_buf, value_buf, gate_buf, beta_buf, decay_buf, decay_ref, bias_ref,
@@ -282,9 +280,7 @@
             place(window_key, h, old_key, key)
             place(window_value, h, old_value[:, half], value[:, half])
             keep(2 * KEYS + h, old_value[:, half], value[:, half])
-            scaled = gate[:, half] * gain_buf[...]
-            spread(early_gate_ref, 0, h, scaled[: 2 * ROWS])
-            spread(late_gate_ref, 0, h, scaled[2 * ROWS :])
+            spread(gate_ref, 0, h, gate[:, half] * gain_buf[...])
 
     late = (history + 2 * ROWS) * HEADS
     late_query_ref[...] = window_query[late:, :].astype(bf16)
@@ -308,9 +304,9 @@
 
 
 def send_kernel(
-    parent_ref, vector_ref, value_ref, strength_ref, forget_ref, gate_ref, tails_ref, state,
-    slots, normed_ref,
-    state_buf, stored_buf, found_buf, normed_buf, update_buf, wanted_buf, wanted_ref,
+    parent_ref, vector_ref, value_ref, strength_ref, forget_ref, tails_ref, state,
+    slots, normed_buf,
+    state_buf, stored_buf, found_buf, update_buf, wanted_buf, wanted_ref,
     look_sem, state_sem, slot_sem,
 ):
     count = slots.shape[0]
@@ -342,7 +338,7 @@
         recall(rows, memory, vector_ref, found_buf)
         for first in range(start, start + SHIP, CHUNK):
             finish(
-                first, strength_ref, forget_ref, gate_ref,
+                first, strength_ref, forget_ref,
                 vector_ref, value_ref, found_buf, normed_buf, update_buf,
             )
         write_rows(rows, update_buf, memory, stored_buf)
@@ -360,8 +356,6 @@
             return carry
 
         lax.fori_loop(0, count, begin, 0, unroll=4)
-    flatten_heads(normed_buf, normed_ref)
-
     def end(slot, carry):
         @pl.when(wanted_ref[slot, 0, 0] >= 0)
         def _():
@@ -373,7 +367,8 @@
 
 
 def second_kernel(
-    parent_ref, late_query, late_key, late_value, late_strength, late_forget, late_gate, conv_ref, early_ref, slots, w_out,
+    parent_ref, late_query, late_key, late_value, late_strength, late_forget, gate_ref, conv_ref,
+    early_ref, slots, w_out,
     *refs,
 ):
     sums = refs[:PARTS]
@@ -409,6 +404,7 @@
     for shift in range(PARTS):
         load_out(shift).start()
     wide = widening()
+    flatten_heads(early_ref, gate_ref, 0, normed_ref)
     for row in range(ROWS):
         load_tail(row).wait()
     for row in range(ROWS):
@@ -441,11 +437,10 @@
     lax.fori_loop(0, ROWS // LATE, group, 0)
     for first in range(0, ROWS, CHUNK):
         finish(
-            first, late_strength, late_forget, late_gate,
+            first, late_strength, late_forget,
             vector_buf, value_buf, found_buf, normed_buf, update_ref,
         )
-    normed_ref[: 2 * ROWS, :] = early_ref[...]
-    flatten_heads(normed_buf, normed_ref.at[2 * ROWS :])
+    flatten_heads(normed_buf, gate_ref, 2 * ROWS, normed_ref)
     for shift in range(PARTS):
         load_out(shift).wait()
     normed = normed_ref[...]
@@ -526,10 +521,11 @@
     return pl.pallas_call(
         first_kernel,
         in_specs=[HBM] * len(arrays),
-        out_specs=[VMEM] * 14,
+        out_specs=[VMEM] * 13,
         out_shape=(
             *[shape((half * HEADS, DV), bf16)] * 3,
-            *[shape((half * HEADS, DV), f32)] * 6,
+            *[shape((half * HEADS, DV), f32)] * 4,
+            shape((rows * HEADS, DV), f32),
             shape((half, SLIM * DV), bf16),
             shape((ROWS, (TAPS - 1) * SLIM, DV), bf16),
             shape((3, TAPS, HEADS, DV), f32),
@@ -555,20 +551,19 @@
 
 def fill_slots(parents, early, tails, state):
     count = parents.shape[0]
-    _, _, found, normed = work_buffers()
+    _, _, found, _ = work_buffers()
     return pl.pallas_call(
         send_kernel,
-        in_specs=[VMEM] * 7 + [HBM],
+        in_specs=[VMEM] * 6 + [HBM],
         out_specs=[HBM, VMEM],
         out_shape=(
             shape((count, SLOT, DV), bf16),
-            shape((2 * ROWS, HEADS * DV), bf16),
+            shape((2 * ROWS * HEADS, DV), f32),
         ),
         scratch_shapes=[
             buffer(state),
             pltpu.VMEM((ROWS, SLOT, DV), bf16),
             found,
-            normed,
             pltpu.VMEM((ROWS, 5 * HEADS, DV), f32),
             pltpu.VMEM((count, 1, DV), jnp.int32),
             pltpu.SMEM((count, 1, DV), jnp.int32),
@@ -581,9 +576,9 @@
     )(parents, *early, tails, in_hbm(state))
 
 
-def second_half(parents, late, conv, normed, slots, w_out):
+def second_half(parents, late, conv, early, slots, w_out):
     window = pltpu.VMEM(((TAPS - 1) * ROWS * HEADS, DV), f32)
-    rows, width = 2 * normed.shape[0], w_out.shape[1] // PARTS
+    rows, width = 4 * ROWS, w_out.shape[1] // PARTS
     *sums, update, last, memory = pl.pallas_call(
         second_kernel,
         in_specs=[SMEM] + [VMEM] * 8 + [HBM] * 2,
@@ -602,14 +597,14 @@
             window,
             *work_buffers(),
             pltpu.VMEM((PARTS, w_out.shape[0], width), bf16),
-            pltpu.VMEM((rows, normed.shape[1]), bf16),
+            pltpu.VMEM((rows, HEADS * DV), bf16),
             pltpu.SemaphoreType.DMA((ROWS,)),
             pltpu.SemaphoreType.DMA((ROWS,)),
             pltpu.SemaphoreType.DMA((PARTS,)),
         ],
         compiler_params=PARAMS,
         name="second_half",
-    )(parents, *late, conv, normed, in_hbm(slots), in_hbm(w_out))
+    )(parents, *late, conv, early, in_hbm(slots), in_hbm(w_out))
     return sums, update, last, memory
 
 
@@ -634,7 +629,7 @@
 
 def sum_heads(blocks):
     total = blocks[0]
-    for shift in (1, 3, 2):
+    for shift in (2, 1, 3):
         pairs = [(i, (i + shift) % PARTS) for i in range(PARTS)]
         total = total + lax.ppermute(blocks[shift], "tensor", pairs).astype(f32)
     return total.astype(bf16)
@@ -688,11 +683,11 @@
             dt_bias,
         )
     )
-    shipped, normed = fill_slots(asked, (vectors, values, *scales[:3]), stored_tails, flat_state)
+    shipped, early = fill_slots(asked, (vectors, values, *scales[:2]), stored_tails, flat_state)
     arrived = lax.all_to_all(shipped, "branch", split_axis=0, concat_axis=0, tiled=True)
-    late = (late_query, late_key, late_value, *scales[3:])
+    late = (late_query, late_key, late_value, *scales[2:])
     sums, update, last, memory = second_half(
-        parents, late, conv, normed, arrived, w_out
+        parents, late, conv, early, arrived, w_out
     )
     out_rows = sum_heads(sums).reshape(inputs.shape[0], ROWS, -1)
     final_state, *final_tails = last_memory(update, last, raw, memory)

time: 147 us -> 148 us (level)
  transfers between devices with their start and end apart: 4 -> 4, of which waited for: 2 -> 1; matrix products, arithmetic and copies ran while one was open for 0% -> 0% of each run, Pallas kernels for 7% -> 7%
where the time goes in v5:
time: 148 us; the launch traced here: 147 us
  blocking collectives  108 us (73%)
  Pallas kernels  20.9 us (14%)
  starting transfers between devices  14.8 us (10%)
    all_to_all x1, blocking collectives, per_device(): lax.all_to_all(shipped, 'branch', split_axis=0, concat_axis=0, tiled=True)  108 us
    all_to_all x1, starting transfers between devices, per_device(): lax.all_to_all(asked, 'branch', split_axis=0, concat_axis=0, tiled=True)  8.24 us
    pallas_call x1, Pallas kernels, first_half(): pl.pallas_call(first_kernel, in_specs=[HBM] * len(arrays), out_specs=[VME...  6.91 us
    ppermute x3, starting transfers between devices, sum_heads(): total = total + lax.ppermute(blocks[shift], 'tensor', pairs).astype(f32)  6.52 us
    pallas_call x1, Pallas kernels, second_half(): pl.pallas_call(second_kernel, in_specs=[SMEM] + [VMEM] * 8 + [HBM] * 2, o...  5.94 us
    pallas_call x1, Pallas kernels, fill_slots(): pl.pallas_call(send_kernel, in_specs=[VMEM] * 6 + [HBM], out_specs=[HBM,...  5.03 us
    pallas_call x1, Pallas kernels, last_memory(): pl.pallas_call(final_kernel, in_specs=[VMEM] * 4, out_specs=[HBM] * 4, ou...  3.06 us
  transfers between devices with their start and end apart: 4, of which 1 were waited for; matrix products, arithmetic and copies ran while one was open for 0% of the time, Pallas kernels for 7%

profile of v5, /device:TPU:0, one launch (start us, length us, event | category | flops | bytes accessed | tf_op | source)
XLA Modules:
  0.0 146.8 jit_solution(9378202941058851799)
XLA Ops:
  0.6 1.3 broadcast_in_dim.10
  1.9 8.2 %all-to-all-start = ((s32[32,1,16]{2,1,0:T(1,128)}), s32[32,1,16]{2,1,0:T(1,128)S(1)}, u32[]{:S(2)}, u32[]{:S(2)}) async-start(s32[32,1,16]{2,1,0:T(1,128)} %broadcast_in_dim.10), calls=%async_computation | async-start | bytes 32768 | tf_op jit(solution)/shard_map/all_to_all | solution.py:661
  10.2 6.9 %first_half.1 = (bf16[256,128]{1,0:T(8,128)(2,1)S(1)}, bf16[256,128]{1,0:T(8,128)(2,1)S(1)}, bf16[256,128]{1,0:T(8,128)(2,1)S(1)}, f32[256,128]{1,0:T(8,128)S(1)...) custom-call(bf16[64,2048]{1,0:T(8,128)(2,1)} %bitcast.14, ...), custom_call_target="tpu_custom_call" | custom-call | tf_op jit(solution)/shard_map/first_half/pallas_call | solution.py:521
  17.1 0.4 all-to-all-done.parent_ref
  17.4 5.0 %fill_slots.1 = (bf16[32,1072,128]{2,1,0:T(8,128)(2,1)}, f32[256,128]{1,0:T(8,128)S(1)}) custom-call(s32[32,1,16]{2,1,0:T(1,128)S(1)} %all-to-all-done.parent_ref, f32[16,32,128]{2,1,0:T(8,128)S(1)} %get-tuple-element.38.vector_ref, f32[2,16,8,128]{3,2,1,0:T(8,128)S(1)} %get-tuple-element.39.value_ref, f32[256,128]{1,0:T(8,128)S(1)} %get-tuple-element.40.strength_ref, ...), custom_call_target="tpu_custom_call" | custom-call | tf_op jit(solution)/shard_map/fill_slots/pallas_call | solution.py:555
  22.5 0.0 copy-start
  22.5 108.1 %all_to_all.10.slots = bf16[32,1072,128]{2,1,0:T(8,128)(2,1)} all-to-all(bf16[32,1072,128]{2,1,0:T(8,128)(2,1)} %get-tuple-element.44), channel_id=1, replica_groups=mesh['branch'=32,'tensor'=4] {'branch'}, dimensions={0} | all-to-all | bytes 17563648 | tf_op jit(solution)/shard_map/all_to_all | solution.py:687
  130.6 0.0 copy-done
  130.6 5.9 %second_half.1 = (f32[64,512]{1,0:T(8,128)S(1)}, bf16[64,512]{1,0:T(8,128)(2,1)S(1)}, bf16[64,512]{1,0:T(8,128)(2,1)S(1)}, bf16[64,512]{1,0:T(8,128)(2,1)S(1)}, ...) custom-call(s32[16]{0:T(128)S(1)} %copy-done, ...), custom_call_target="tpu_custom_call" | custom-call | tf_op jit(solution)/shard_map/second_half/pallas_call | solution.py:582
  136.6 3.3 %collective-permute-start = (bf16[64,512]{1,0:T(8,128)(2,1)S(1)}, bf16[64,512]{1,0:T(8,128)(2,1)S(1)}, u32[]{:S(2)}, u32[]{:S(2)}) collective-permute-start(bf16[64,512]{1,0:T(8,128)(2,1)S(1)} %get-tuple-element.46), channel_id=1, source_target_pairs={{0,2},{1,3},{2,0},{3,1},{4,6},{5,7},{6,4},{7,5},{8,10},{9,11},{10,... | collective-permute-start | bytes 196616 | tf_op jit(solution)/shard_map/ppermute | solution.py:634
  139.8 0.7 collective-permute-start.1
  140.5 2.6 %collective-permute-start.2 = (bf16[64,512]{1,0:T(8,128)(2,1)S(1)}, bf16[64,512]{1,0:T(8,128)(2,1)S(1)}, u32[]{:S(2)}, u32[]{:S(2)}) collective-permute-start(bf16[64,512]{1,0:T(8,128)(2,1)S(1)} %get-tuple-element.48), channel_id=1, source_target_pairs={{0,3},{1,0},{2,1},{3,2},{4,7},{5,4},{6,5},{7,6},{8,11},{9,8},{10,9... | collective-permute-start | bytes 196616 | tf_op jit(solution)/shard_map/ppermute | solution.py:634
  143.1 3.1 %last_memory.1 = (bf16[16,1024,128]{2,1,0:T(8,128)(2,1)}, bf16[3,16,512]{2,1,0:T(8,128)(2,1)}, bf16[3,16,512]{2,1,0:T(8,128)(2,1)}, bf16[3,16,1024]{2,1,0:T(8,128)(2,1)}) custom-call(f32[16,40,128]{2,1,0:T(8,128)S(1)} %get-tuple-element.49.update_ref, bf16[16,16,128]{2,1,0:T(8,128)(2,1)S(1)} %get-tuple-element.50.last_ref, ...), custom_call_target="tpu_custom_call" | custom-call | tf_op jit(solution)/shard_map/last_memory/pallas_call | solution.py:613
  146.1 0.0 collective-permute-done
  146.2 0.0 collective-permute-done.1
  146.2 0.0 collective-permute-done.2
  146.2 0.7 add_convert_fusion
Async XLA Ops:
  1.9 15.5 %all-to-all-start = ((s32[32,1,16]{2,1,0:T(1,128)}), s32[32,1,16]{2,1,0:T(1,128)S(1)}, u32[]{:S(2)}, u32[]{:S(2)}) async-start(s32[32,1,16]{2,1,0:T(1,128)} %broadcast_in_dim.10), calls=%async_computation | async-start | bytes 32768 | tf_op jit(solution)/shard_map/all_to_all | solution.py:661
  22.5 108.1 %copy-start = (s32[16]{0:T(128)S(1)}, s32[16]{0:T(128)}, u32[]{:S(2)}) copy-start(s32[16]{0:T(128)} %parent_ref.1) | copy-start | bytes 196
  136.6 9.6 %collective-permute-start = (bf16[64,512]{1,0:T(8,128)(2,1)S(1)}, bf16[64,512]{1,0:T(8,128)(2,1)S(1)}, u32[]{:S(2)}, u32[]{:S(2)}) collective-permute-start(bf16[64,512]{1,0:T(8,128)(2,1)S(1)} %get-tuple-element.46), channel_id=1, source_target_pairs={{0,2},{1,3},{2,0},{3,1},{4,6},{5,7},{6,4},{7,5},{8,10},{9,11},{10,... | collective-permute-start | bytes 196616 | tf_op jit(solution)/shard_map/ppermute | solution.py:634
  139.8 6.3 %collective-permute-start.1 = (bf16[64,512]{1,0:T(8,128)(2,1)S(1)}, bf16[64,512]{1,0:T(8,128)(2,1)S(1)}, u32[]{:S(2)}, u32[]{:S(2)}) collective-permute-start(bf16[64,512]{1,0:T(8,128)(2,1)S(1)} %get-tuple-element.47), channel_id=1, source_target_pairs={{0,1},{1,2},{2,3},{3,0},{4,5},{5,6},{6,7},{7,4},{8,9},{9,10},{10,1... | collective-permute-start | bytes 196616 | tf_op jit(solution)/shard_map/ppermute | solution.py:634
  140.5 5.7 %collective-permute-start.2 = (bf16[64,512]{1,0:T(8,128)(2,1)S(1)}, bf16[64,512]{1,0:T(8,128)(2,1)S(1)}, u32[]{:S(2)}, u32[]{:S(2)}) collective-permute-start(bf16[64,512]{1,0:T(8,128)(2,1)S(1)} %get-tuple-element.48), channel_id=1, source_target_pairs={{0,3},{1,0},{2,1},{3,2},{4,7},{5,4},{6,5},{7,6},{8,11},{9,8},{10,9... | collective-permute-start | bytes 196616 | tf_op jit(solution)/shard_map/ppermute | solution.py:634

commit v6 on v5

--- a/solution.py
+++ b/solution.py
@@ -21,7 +21,7 @@
 GROUP = 8
 LATE = 16
 AHEAD = 2
-SHIP = 8
+SHIP = 4
 f32 = jnp.float32
 bf16 = jnp.bfloat16
 
@@ -355,7 +355,7 @@
 
             return carry
 
-        lax.fori_loop(0, count, begin, 0, unroll=4)
+        lax.fori_loop(0, count, begin, 0, unroll=count)
     def end(slot, carry):
         @pl.when(wanted_ref[slot, 0, 0] >= 0)
         def _():
@@ -363,7 +363,7 @@
 
         return carry
 
-    lax.fori_loop(0, count, end, 0, unroll=4)
+    lax.fori_loop(0, count, end, 0, unroll=count)
 
 
 def second_kernel(
@@ -629,7 +629,7 @@
 
 def sum_heads(blocks):
     total = blocks[0]
-    for shift in (2, 1, 3):
+    for shift in (1, 3, 2):
         pairs = [(i, (i + shift) % PARTS) for i in range(PARTS)]
         total = total + lax.ppermute(blocks[shift], "tensor", pairs).astype(f32)
     return total.astype(bf16)

time: 148 us -> 146 us (0.986)
  transfers between devices with their start and end apart: 4 -> 4, of which waited for: 1 -> 2; matrix products, arithmetic and copies ran while one was open for 0% -> 0% of each run, Pallas kernels for 7% -> 7%
where the time goes in v6:
time: 146 us
  blocking collectives  108 us (74%)
  Pallas kernels  20.5 us (14%)
  starting transfers between devices  13.6 us (9%)
    all_to_all x1, blocking collectives, per_device(): lax.all_to_all(shipped, 'branch', split_axis=0, concat_axis=0, tiled=True)  108 us
    all_to_all x1, starting transfers between devices, per_device(): lax.all_to_all(asked, 'branch', split_axis=0, concat_axis=0, tiled=True)  8.24 us
    pallas_call x1, Pallas kernels, first_half(): pl.pallas_call(first_kernel, in_specs=[HBM] * len(arrays), out_specs=[VME...  6.91 us
    pallas_call x1, Pallas kernels, second_half(): pl.pallas_call(second_kernel, in_specs=[SMEM] + [VMEM] * 8 + [HBM] * 2, o...  5.94 us
    ppermute x3, starting transfers between devices, sum_heads(): total = total + lax.ppermute(blocks[shift], 'tensor', pairs).astype(f32)  5.34 us
    pallas_call x1, Pallas kernels, fill_slots(): pl.pallas_call(send_kernel, in_specs=[VMEM] * 6 + [HBM], out_specs=[HBM,...  4.62 us
    pallas_call x1, Pallas kernels, last_memory(): pl.pallas_call(final_kernel, in_specs=[VMEM] * 4, out_specs=[HBM] * 4, ou...  3.06 us
  transfers between devices with their start and end apart: 4, of which 2 were waited for; matrix products, arithmetic and copies ran while one was open for 0% of the time, Pallas kernels for 7%

profile of v6, /device:TPU:0, one launch (start us, length us, event | category | flops | bytes accessed | tf_op | source)
XLA Modules:
  0.0 146.2 jit_solution(11525258545978849392)
XLA Ops:
  0.6 1.3 broadcast_in_dim.10
  1.9 8.2 %all-to-all-start = ((s32[32,1,16]{2,1,0:T(1,128)}), s32[32,1,16]{2,1,0:T(1,128)S(1)}, u32[]{:S(2)}, u32[]{:S(2)}) async-start(s32[32,1,16]{2,1,0:T(1,128)} %broadcast_in_dim.10), calls=%async_computation | async-start | bytes 32768 | tf_op jit(solution)/shard_map/all_to_all | solution.py:661
  10.2 6.9 %first_half.1 = (bf16[256,128]{1,0:T(8,128)(2,1)S(1)}, bf16[256,128]{1,0:T(8,128)(2,1)S(1)}, bf16[256,128]{1,0:T(8,128)(2,1)S(1)}, f32[256,128]{1,0:T(8,128)S(1)...) custom-call(bf16[64,2048]{1,0:T(8,128)(2,1)} %bitcast.14, ...), custom_call_target="tpu_custom_call" | custom-call | tf_op jit(solution)/shard_map/first_half/pallas_call | solution.py:521
  17.1 0.4 all-to-all-done.parent_ref
  17.4 4.6 %fill_slots.1 = (bf16[32,1072,128]{2,1,0:T(8,128)(2,1)}, f32[256,128]{1,0:T(8,128)S(1)}) custom-call(s32[32,1,16]{2,1,0:T(1,128)S(1)} %all-to-all-done.parent_ref, f32[16,32,128]{2,1,0:T(8,128)S(1)} %get-tuple-element.38.vector_ref, f32[2,16,8,128]{3,2,1,0:T(8,128)S(1)} %get-tuple-element.39.value_ref, f32[256,128]{1,0:T(8,128)S(1)} %get-tuple-element.40.strength_ref, ...), custom_call_target="tpu_custom_call" | custom-call | tf_op jit(solution)/shard_map/fill_slots/pallas_call | solution.py:555
  22.1 0.0 copy-start
  22.1 108.4 %all_to_all.10.slots = bf16[32,1072,128]{2,1,0:T(8,128)(2,1)} all-to-all(bf16[32,1072,128]{2,1,0:T(8,128)(2,1)} %get-tuple-element.44), channel_id=1, replica_groups=mesh['branch'=32,'tensor'=4] {'branch'}, dimensions={0} | all-to-all | bytes 17563648 | tf_op jit(solution)/shard_map/all_to_all | solution.py:687
  130.5 0.0 copy-done
  130.5 5.9 %second_half.1 = (f32[64,512]{1,0:T(8,128)S(1)}, bf16[64,512]{1,0:T(8,128)(2,1)S(1)}, bf16[64,512]{1,0:T(8,128)(2,1)S(1)}, bf16[64,512]{1,0:T(8,128)(2,1)S(1)}, ...) custom-call(s32[16]{0:T(128)S(1)} %copy-done, ...), custom_call_target="tpu_custom_call" | custom-call | tf_op jit(solution)/shard_map/second_half/pallas_call | solution.py:582
  136.4 1.6 %collective-permute-start = (bf16[64,512]{1,0:T(8,128)(2,1)S(1)}, bf16[64,512]{1,0:T(8,128)(2,1)S(1)}, u32[]{:S(2)}, u32[]{:S(2)}) collective-permute-start(bf16[64,512]{1,0:T(8,128)(2,1)S(1)} %get-tuple-element.46), channel_id=1, source_target_pairs={{0,1},{1,2},{2,3},{3,0},{4,5},{5,6},{6,7},{7,4},{8,9},{9,10},{10,1... | collective-permute-start | bytes 196616 | tf_op jit(solution)/shard_map/ppermute | solution.py:634
  138.1 1.7 %collective-permute-start.1 = (bf16[64,512]{1,0:T(8,128)(2,1)S(1)}, bf16[64,512]{1,0:T(8,128)(2,1)S(1)}, u32[]{:S(2)}, u32[]{:S(2)}) collective-permute-start(bf16[64,512]{1,0:T(8,128)(2,1)S(1)} %get-tuple-element.47), channel_id=1, source_target_pairs={{0,3},{1,0},{2,1},{3,2},{4,7},{5,4},{6,5},{7,6},{8,11},{9,8},{10,9... | collective-permute-start | bytes 196616 | tf_op jit(solution)/shard_map/ppermute | solution.py:634
  139.7 2.0 %collective-permute-start.2 = (bf16[64,512]{1,0:T(8,128)(2,1)S(1)}, bf16[64,512]{1,0:T(8,128)(2,1)S(1)}, u32[]{:S(2)}, u32[]{:S(2)}) collective-permute-start(bf16[64,512]{1,0:T(8,128)(2,1)S(1)} %get-tuple-element.48), channel_id=1, source_target_pairs={{0,2},{1,3},{2,0},{3,1},{4,6},{5,7},{6,4},{7,5},{8,10},{9,11},{10,... | collective-permute-start | bytes 196616 | tf_op jit(solution)/shard_map/ppermute | solution.py:634
  141.8 3.1 %last_memory.1 = (bf16[16,1024,128]{2,1,0:T(8,128)(2,1)}, bf16[3,16,512]{2,1,0:T(8,128)(2,1)}, bf16[3,16,512]{2,1,0:T(8,128)(2,1)}, bf16[3,16,1024]{2,1,0:T(8,128)(2,1)}) custom-call(f32[16,40,128]{2,1,0:T(8,128)S(1)} %get-tuple-element.49.update_ref, bf16[16,16,128]{2,1,0:T(8,128)(2,1)S(1)} %get-tuple-element.50.last_ref, ...), custom_call_target="tpu_custom_call" | custom-call | tf_op jit(solution)/shard_map/last_memory/pallas_call | solution.py:613
  144.8 0.0 collective-permute-done
  144.8 0.0 collective-permute-done.1
  144.9 0.6 collective-permute-done.2
  145.5 0.7 add_convert_fusion
Async XLA Ops:
  1.9 15.5 %all-to-all-start = ((s32[32,1,16]{2,1,0:T(1,128)}), s32[32,1,16]{2,1,0:T(1,128)S(1)}, u32[]{:S(2)}, u32[]{:S(2)}) async-start(s32[32,1,16]{2,1,0:T(1,128)} %broadcast_in_dim.10), calls=%async_computation | async-start | bytes 32768 | tf_op jit(solution)/shard_map/all_to_all | solution.py:661
  22.1 108.4 %copy-start = (s32[16]{0:T(128)S(1)}, s32[16]{0:T(128)}, u32[]{:S(2)}) copy-start(s32[16]{0:T(128)} %parent_ref.1) | copy-start | bytes 196
  136.4 8.4 %collective-permute-start = (bf16[64,512]{1,0:T(8,128)(2,1)S(1)}, bf16[64,512]{1,0:T(8,128)(2,1)S(1)}, u32[]{:S(2)}, u32[]{:S(2)}) collective-permute-start(bf16[64,512]{1,0:T(8,128)(2,1)S(1)} %get-tuple-element.46), channel_id=1, source_target_pairs={{0,1},{1,2},{2,3},{3,0},{4,5},{5,6},{6,7},{7,4},{8,9},{9,10},{10,1... | collective-permute-start | bytes 196616 | tf_op jit(solution)/shard_map/ppermute | solution.py:634
  138.1 6.8 %collective-permute-start.1 = (bf16[64,512]{1,0:T(8,128)(2,1)S(1)}, bf16[64,512]{1,0:T(8,128)(2,1)S(1)}, u32[]{:S(2)}, u32[]{:S(2)}) collective-permute-start(bf16[64,512]{1,0:T(8,128)(2,1)S(1)} %get-tuple-element.47), channel_id=1, source_target_pairs={{0,3},{1,0},{2,1},{3,2},{4,7},{5,4},{6,5},{7,6},{8,11},{9,8},{10,9... | collective-permute-start | bytes 196616 | tf_op jit(solution)/shard_map/ppermute | solution.py:634
  139.7 5.8 %collective-permute-start.2 = (bf16[64,512]{1,0:T(8,128)(2,1)S(1)}, bf16[64,512]{1,0:T(8,128)(2,1)S(1)}, u32[]{:S(2)}, u32[]{:S(2)}) collective-permute-start(bf16[64,512]{1,0:T(8,128)(2,1)S(1)} %get-tuple-element.48), channel_id=1, source_target_pairs={{0,2},{1,3},{2,0},{3,1},{4,6},{5,7},{6,4},{7,5},{8,10},{9,11},{10,... | collective-permute-start | bytes 196616 | tf_op jit(solution)/shard_map/ppermute | solution.py:634

commit v7 on v6

--- a/solution.py
+++ b/solution.py
@@ -314,7 +314,7 @@
     def load(row):
         return pltpu.make_async_copy(state.at[row], state_buf.at[row], state_sem.at[row])
 
-    for row in range(ROWS):
+    for row in range(2 * SHIP):
         load(row).start()
     parent = parent_ref[...]
     mine = parent // ROWS == lax.axis_index("branch")
@@ -335,6 +335,8 @@
         rows = range(start, start + SHIP)
         for row in rows:
             load(row).wait()
+        for row in range(start + 2 * SHIP, min(start + 3 * SHIP, ROWS)):
+            load(row).start()
         recall(rows, memory, vector_ref, found_buf)
         for first in range(start, start + SHIP, CHUNK):
             finish(
@@ -401,8 +403,6 @@
             w_out.at[:, pl.ds(start, width)], out_buf.at[shift], out_sem.at[shift]
         )
 
-    for shift in range(PARTS):
-        load_out(shift).start()
     wide = widening()
     flatten_heads(early_ref, gate_ref, 0, normed_ref)
     for row in range(ROWS):
@@ -426,6 +426,8 @@
         return part_of(fresh[kind], tap - (TAPS - 1), first, CHUNK).astype(f32)
 
     find_vectors(window, conv_ref, vector_buf, value_buf)
+    for shift in range(PARTS):
+        load_out(shift).start()
 
     def group(index, carry):
         rows = [index * LATE + i for i in range(LATE)]

time: 146 us -> 147 us (level)
  no operation moved by 1% of the time
where the time goes in v7:
time: 147 us
  blocking collectives  108 us (73%)
  Pallas kernels  21.8 us (15%)
  starting transfers between devices  13.5 us (9%)
    all_to_all x1, blocking collectives, per_device(): lax.all_to_all(shipped, 'branch', split_axis=0, concat_axis=0, tiled=True)  108 us
    all_to_all x1, starting transfers between devices, per_device(): lax.all_to_all(asked, 'branch', split_axis=0, concat_axis=0, tiled=True)  8.24 us
    pallas_call x1, Pallas kernels, first_half(): pl.pallas_call(first_kernel, in_specs=[HBM] * len(arrays), out_specs=[VME...  6.91 us
    pallas_call x1, Pallas kernels, second_half(): pl.pallas_call(second_kernel, in_specs=[SMEM] + [VMEM] * 8 + [HBM] * 2, o...  6.23 us
    pallas_call x1, Pallas kernels, fill_slots(): pl.pallas_call(send_kernel, in_specs=[VMEM] * 6 + [HBM], out_specs=[HBM,...  5.57 us
    ppermute x3, starting transfers between devices, sum_heads(): total = total + lax.ppermute(blocks[shift], 'tensor', pairs).astype(f32)  5.29 us
    pallas_call x1, Pallas kernels, last_memory(): pl.pallas_call(final_kernel, in_specs=[VMEM] * 4, out_specs=[HBM] * 4, ou...  3.06 us
  transfers between devices with their start and end apart: 4, of which 2 were waited for; matrix products, arithmetic and copies ran while one was open for 0% of the time, Pallas kernels for 7%

profile of v7, /device:TPU:0, one launch (start us, length us, event | category | flops | bytes accessed | tf_op | source)
XLA Modules:
  0.0 146.9 jit_solution(1820707958235411919)
XLA Ops:
  0.6 1.3 broadcast_in_dim.10
  1.9 8.2 %all-to-all-start = ((s32[32,1,16]{2,1,0:T(1,128)}), s32[32,1,16]{2,1,0:T(1,128)S(1)}, u32[]{:S(2)}, u32[]{:S(2)}) async-start(s32[32,1,16]{2,1,0:T(1,128)} %broadcast_in_dim.10), calls=%async_computation | async-start | bytes 32768 | tf_op jit(solution)/shard_map/all_to_all | solution.py:663
  10.2 6.9 %first_half.1 = (bf16[256,128]{1,0:T(8,128)(2,1)S(1)}, bf16[256,128]{1,0:T(8,128)(2,1)S(1)}, bf16[256,128]{1,0:T(8,128)(2,1)S(1)}, f32[256,128]{1,0:T(8,128)S(1)...) custom-call(bf16[64,2048]{1,0:T(8,128)(2,1)} %bitcast.14, ...), custom_call_target="tpu_custom_call" | custom-call | tf_op jit(solution)/shard_map/first_half/pallas_call | solution.py:523
  17.1 0.4 all-to-all-done.parent_ref
  17.4 5.6 %fill_slots.1 = (bf16[32,1072,128]{2,1,0:T(8,128)(2,1)}, f32[256,128]{1,0:T(8,128)S(1)}) custom-call(s32[32,1,16]{2,1,0:T(1,128)S(1)} %all-to-all-done.parent_ref, f32[16,32,128]{2,1,0:T(8,128)S(1)} %get-tuple-element.38.vector_ref, f32[2,16,8,128]{3,2,1,0:T(8,128)S(1)} %get-tuple-element.39.value_ref, f32[256,128]{1,0:T(8,128)S(1)} %get-tuple-element.40.strength_ref, ...), custom_call_target="tpu_custom_call" | custom-call | tf_op jit(solution)/shard_map/fill_slots/pallas_call | solution.py:557
  23.0 0.0 copy-start
  23.0 107.9 %all_to_all.10.slots = bf16[32,1072,128]{2,1,0:T(8,128)(2,1)} all-to-all(bf16[32,1072,128]{2,1,0:T(8,128)(2,1)} %get-tuple-element.44), channel_id=1, replica_groups=mesh['branch'=32,'tensor'=4] {'branch'}, dimensions={0} | all-to-all | bytes 17563648 | tf_op jit(solution)/shard_map/all_to_all | solution.py:689
  130.9 0.0 copy-done
  130.9 6.2 %second_half.1 = (f32[64,512]{1,0:T(8,128)S(1)}, bf16[64,512]{1,0:T(8,128)(2,1)S(1)}, bf16[64,512]{1,0:T(8,128)(2,1)S(1)}, bf16[64,512]{1,0:T(8,128)(2,1)S(1)}, ...) custom-call(s32[16]{0:T(128)S(1)} %copy-done, ...), custom_call_target="tpu_custom_call" | custom-call | tf_op jit(solution)/shard_map/second_half/pallas_call | solution.py:584
  137.2 1.6 %collective-permute-start = (bf16[64,512]{1,0:T(8,128)(2,1)S(1)}, bf16[64,512]{1,0:T(8,128)(2,1)S(1)}, u32[]{:S(2)}, u32[]{:S(2)}) collective-permute-start(bf16[64,512]{1,0:T(8,128)(2,1)S(1)} %get-tuple-element.46), channel_id=1, source_target_pairs={{0,1},{1,2},{2,3},{3,0},{4,5},{5,6},{6,7},{7,4},{8,9},{9,10},{10,1... | collective-permute-start | bytes 196616 | tf_op jit(solution)/shard_map/ppermute | solution.py:636
  138.8 1.7 %collective-permute-start.1 = (bf16[64,512]{1,0:T(8,128)(2,1)S(1)}, bf16[64,512]{1,0:T(8,128)(2,1)S(1)}, u32[]{:S(2)}, u32[]{:S(2)}) collective-permute-start(bf16[64,512]{1,0:T(8,128)(2,1)S(1)} %get-tuple-element.47), channel_id=1, source_target_pairs={{0,3},{1,0},{2,1},{3,2},{4,7},{5,4},{6,5},{7,6},{8,11},{9,8},{10,9... | collective-permute-start | bytes 196616 | tf_op jit(solution)/shard_map/ppermute | solution.py:636
  140.5 2.0 %collective-permute-start.2 = (bf16[64,512]{1,0:T(8,128)(2,1)S(1)}, bf16[64,512]{1,0:T(8,128)(2,1)S(1)}, u32[]{:S(2)}, u32[]{:S(2)}) collective-permute-start(bf16[64,512]{1,0:T(8,128)(2,1)S(1)} %get-tuple-element.48), channel_id=1, source_target_pairs={{0,2},{1,3},{2,0},{3,1},{4,6},{5,7},{6,4},{7,5},{8,10},{9,11},{10,... | collective-permute-start | bytes 196616 | tf_op jit(solution)/shard_map/ppermute | solution.py:636
  142.5 3.1 %last_memory.1 = (bf16[16,1024,128]{2,1,0:T(8,128)(2,1)}, bf16[3,16,512]{2,1,0:T(8,128)(2,1)}, bf16[3,16,512]{2,1,0:T(8,128)(2,1)}, bf16[3,16,1024]{2,1,0:T(8,128)(2,1)}) custom-call(f32[16,40,128]{2,1,0:T(8,128)S(1)} %get-tuple-element.49.update_ref, bf16[16,16,128]{2,1,0:T(8,128)(2,1)S(1)} %get-tuple-element.50.last_ref, ...), custom_call_target="tpu_custom_call" | custom-call | tf_op jit(solution)/shard_map/last_memory/pallas_call | solution.py:615
  145.5 0.0 collective-permute-done
  145.6 0.0 collective-permute-done.1
  145.6 0.7 collective-permute-done.2
  146.3 0.7 add_convert_fusion
Async XLA Ops:
  1.9 15.5 %all-to-all-start = ((s32[32,1,16]{2,1,0:T(1,128)}), s32[32,1,16]{2,1,0:T(1,128)S(1)}, u32[]{:S(2)}, u32[]{:S(2)}) async-start(s32[32,1,16]{2,1,0:T(1,128)} %broadcast_in_dim.10), calls=%async_computation | async-start | bytes 32768 | tf_op jit(solution)/shard_map/all_to_all | solution.py:663
  23.0 107.9 %copy-start = (s32[16]{0:T(128)S(1)}, s32[16]{0:T(128)}, u32[]{:S(2)}) copy-start(s32[16]{0:T(128)} %parent_ref.1) | copy-start | bytes 196
  137.2 8.4 %collective-permute-start = (bf16[64,512]{1,0:T(8,128)(2,1)S(1)}, bf16[64,512]{1,0:T(8,128)(2,1)S(1)}, u32[]{:S(2)}, u32[]{:S(2)}) collective-permute-start(bf16[64,512]{1,0:T(8,128)(2,1)S(1)} %get-tuple-element.46), channel_id=1, source_target_pairs={{0,1},{1,2},{2,3},{3,0},{4,5},{5,6},{6,7},{7,4},{8,9},{9,10},{10,1... | collective-permute-start | bytes 196616 | tf_op jit(solution)/shard_map/ppermute | solution.py:636
  138.8 6.7 %collective-permute-start.1 = (bf16[64,512]{1,0:T(8,128)(2,1)S(1)}, bf16[64,512]{1,0:T(8,128)(2,1)S(1)}, u32[]{:S(2)}, u32[]{:S(2)}) collective-permute-start(bf16[64,512]{1,0:T(8,128)(2,1)S(1)} %get-tuple-element.47), channel_id=1, source_target_pairs={{0,3},{1,0},{2,1},{3,2},{4,7},{5,4},{6,5},{7,6},{8,11},{9,8},{10,9... | collective-permute-start | bytes 196616 | tf_op jit(solution)/shard_map/ppermute | solution.py:636
  140.5 5.8 %collective-permute-start.2 = (bf16[64,512]{1,0:T(8,128)(2,1)S(1)}, bf16[64,512]{1,0:T(8,128)(2,1)S(1)}, u32[]{:S(2)}, u32[]{:S(2)}) collective-permute-start(bf16[64,512]{1,0:T(8,128)(2,1)S(1)} %get-tuple-element.48), channel_id=1, source_target_pairs={{0,2},{1,3},{2,0},{3,1},{4,6},{5,7},{6,4},{7,5},{8,10},{9,11},{10,... | collective-permute-start | bytes 196616 | tf_op jit(solution)/shard_map/ppermute | solution.py:636
